TPU v7x, 128 devices: a whole 4x4x4 slice. The times are simulated.
128 devices in a mesh: comp: 8 (over x, core), cpl: 16 (over y, z).
Axes of the slice: x: 4, y: 4, z: 4, core: 2. Of those that a mesh axis runs over, the one named last changes fastest.
Arguments:
- atm_fields: bfloat16 [16384, 64, 128], P(('comp', 'cpl')), may hold values from -6 to 6
- land_bits: int32 [16384, 5], P(('comp', 'cpl')), may hold values from 0 to 1073741823
- coupler_owner: int32 [16384], P(('comp', 'cpl')), may hold values from 0 to 127, as said below
- tile_col: int32 [32768], P(('comp', 'cpl')), may hold values from 0 to 255, as said below
- tile_row: int32 [32768], P(('comp', 'cpl')), may hold values from -1 to 511, as said below
- tile_weight: bfloat16 [32768, 4, 128], P(('comp', 'cpl')), may hold values from 0.001953125 to 0.03125
- tile_target: int32 [32768, 4, 128], P(('comp', 'cpl')), may hold values from 0 to 127
Outputs:
- merged: float32 [512, 64, 128], P(('comp', 'cpl'))
Inputs may be any that keep to these rules, and one draw needn't show every extreme that they name: `coupler_owner`: of the blocks of one device, at most 2 have one coupler device; in every draw one device receives 2 blocks from every device. `tile_col`: on each device every slot index appears in exactly one tile. `tile_row`: A tile is padding (-1) exactly when its slot is empty. Each ocean block receives exactly 32 tiles, all reading blocks of one atmosphere device; the tiles reading one atmosphere device's blocks add to ocean blocks of one ocean device, a different one for each atmosphere device and never the device itself. So no device holds more than 2 tiles for one ocean device, and in every draw one device holds 2 for every ocean device.
All inputs are finite; a program needn't handle non-finite values.
Results may differ from a plain program's by a relative error of at most 0.00065.
Values may be sent and summed in bfloat16 or wider, within the bound.
No kernel may reach another device: no remote copies, remote signals or barrier semaphores. Data moves between devices by JAX's collectives and lax.ppermute only.
A program may use at most 64 MiB of HBM per device.

v0:
```python
import jax
import jax.numpy as jnp
import numpy as np
from jax import lax
from jax.sharding import PartitionSpec as P

RATIO = 32


drag_coef = 0.5
heat_coef = 0.5
vapor_coef = 0.5


def surface_fluxes(state_fields, packed_bits):
    columns = np.arange(state_fields.shape[2])
    packed = packed_bits[:, columns // 30]
    ocean = jnp.right_shift(packed, jnp.asarray(columns % 30, dtype=jnp.int32)) & 1 == 1
    state = state_fields[:, :6].astype(jnp.float32)
    wind_east = state[:, 0]
    wind_north = state[:, 1]
    wind_speed = jnp.sqrt(wind_east * wind_east + wind_north * wind_north + 0.25)
    bulk = jnp.stack(
        [
            drag_coef * wind_speed * wind_east,
            drag_coef * wind_speed * wind_north,
            heat_coef * wind_speed * (state[:, 4] - state[:, 2]),
            vapor_coef * wind_speed * (state[:, 5] - state[:, 3]),
        ],
        1,
    )
    blended = jnp.where(ocean[:, None, :], bulk, state[:, :4]).astype(jnp.bfloat16)
    return jnp.concatenate([blended, state_fields[:, 4:]], 1)


def slot_positions(targets, valid, target_count, width, overflow):
    onehot = (
        (targets[:, None] == jnp.arange(target_count, dtype=jnp.int32)[None, :]) & valid[:, None]
    ).astype(jnp.int32)
    rank_in = jnp.sum(jnp.cumsum(onehot, 0) * onehot, 1) - 1
    return jnp.where(valid, targets * width + rank_in, overflow)


def remap_group(items):
    block_rows, entry_weights, entry_targets = items
    columns = jnp.arange(block_rows.shape[2], dtype=jnp.int32)
    total = None
    for entry in range(entry_weights.shape[1]):
        dense = jnp.where(
            entry_targets[:, entry, :, None] == columns[None, None, :],
            entry_weights[:, entry, :, None],
            jnp.zeros((), jnp.bfloat16),
        )
        term = jnp.einsum("tfi,tij->tfj", block_rows, dense, preferred_element_type=jnp.float32)
        total = term if total is None else total + term
    return total


def remap_tiles(block_rows, entry_weights, entry_targets):
    count = block_rows.shape[0]
    group = 64 if count % 64 == 0 else count
    shaped = (
        block_rows.reshape((count // group, group) + block_rows.shape[1:]),
        entry_weights.reshape((count // group, group) + entry_weights.shape[1:]),
        entry_targets.reshape((count // group, group) + entry_targets.shape[1:]),
    )
    result = lax.map(remap_group, shaped)
    return result.reshape((count,) + block_rows.shape[1:])


def on_device(atm_fields, land_bits, coupler_owner, tile_col, tile_row, tile_weight, tile_target):
    rank_count = lax.axis_size("comp") * lax.axis_size("cpl")
    atm_blocks = atm_fields.shape[0]
    field_count = atm_fields.shape[1]
    block_cols = atm_fields.shape[2]
    slot_cap = 2 * atm_blocks // rank_count
    ocean_blocks = atm_blocks // RATIO
    slot_total = rank_count * slot_cap
    tile_count = tile_col.shape[0]
    everyone = jnp.ones(coupler_owner.shape, bool)
    home_slot = slot_positions(coupler_owner, everyone, rank_count, slot_cap, slot_total)
    outgoing = (
        jnp.zeros((slot_total, field_count, block_cols), jnp.bfloat16).at[home_slot].set(atm_fields)
    )
    packed_out = jnp.zeros((slot_total, land_bits.shape[1]), jnp.int32).at[home_slot].set(land_bits)
    slot_state, slot_bits = (
        lax.all_to_all(outgoing, ("comp", "cpl"), split_axis=0, concat_axis=0, tiled=True),
        lax.all_to_all(packed_out, ("comp", "cpl"), split_axis=0, concat_axis=0, tiled=True),
    )
    slot_fluxes = surface_fluxes(slot_state, slot_bits)
    picked = jnp.take(slot_fluxes, tile_col, axis=0)
    valid = tile_row >= 0
    ocean_home = jnp.where(valid, tile_row // ocean_blocks, 0)
    send_at = slot_positions(ocean_home, valid, rank_count, slot_cap, tile_count)
    row_out = (
        jnp.full((tile_count,), -1, jnp.int32).at[send_at].set(tile_row % ocean_blocks, mode="drop")
    )
    partial_value = remap_tiles(picked, tile_weight, tile_target)
    partial_out = (
        jnp.zeros(partial_value.shape, jnp.float32).at[send_at].set(partial_value, mode="drop")
    )
    arrived, arrived_rows = (
        lax.all_to_all(partial_out, ("comp", "cpl"), split_axis=0, concat_axis=0, tiled=True),
        lax.all_to_all(row_out, ("comp", "cpl"), split_axis=0, concat_axis=0, tiled=True),
    )
    selector = (arrived_rows[None, :] == jnp.arange(ocean_blocks, dtype=jnp.int32)[:, None]).astype(
        jnp.float32
    )
    return jnp.einsum("ot,tfj->ofj", selector, arrived, precision=lax.Precision.HIGHEST)


def solution(mesh):
    in_specs = (
        P(("comp", "cpl"), None, None),
        P(("comp", "cpl"), None),
        P(("comp", "cpl")),
        P(("comp", "cpl")),
        P(("comp", "cpl")),
        P(("comp", "cpl"), None, None),
        P(("comp", "cpl"), None, None),
    )
    out_specs = P(("comp", "cpl"), None, None)
    return jax.shard_map(
        on_device, mesh=mesh, in_specs=in_specs, out_specs=out_specs, check_vma=False
    )
```

profile of v0, /device:TPU:1, one launch (start us, length us, event | category | flops | bytes accessed | tf_op | source)
XLA Modules:
  0.0 388.7 jit_solution(1008728833888683913)
XLA Ops:
  4.8 11.5 %all-to-all-start.1 = ((s32[128,2,5]{2,1,0:T(2,128)}), s32[128,2,5]{2,1,0:T(2,128)S(1)}, u32[]{:S(2)}, u32[]{:S(2)}) async-start(s32[128,2,5]{2,1,0:T(2,128)} %bitcast.19), calls=%async_computation.1 | async-start | bytes 262144 | tf_op jit(solution)/shard_map/all_to_all | solution.py:88
  19.4 15.7 %scatter_fusion = bf16[256,64,128]{2,1,0:T(8,128)(2,1)} fusion(bf16[256,64,128]{2,1,0:T(8,128)(2,1)} %broadcast_in_dim.125, s32[128]{0:T(128)S(1)} %compare_select_fusion.2, bf16[128,64,128]{2,1,0:T(8,128)(2,1)S(1)} %copy-done.1), kind=kCustom, calls=%fused_computation.4 | custom fusion | bytes 6291968 | tf_op jit(solution)/shard_map/scatter | solution.py:83
  35.1 10.3 %all-to-all-start.2 = ((bf16[256,64,128]{2,1,0:T(8,128)(2,1)}), bf16[256,64,128]{2,1,0:T(8,128)(2,1)}, u32[]{:S(2)}, u32[]{:S(2)}) async-start(bf16[256,64,128]{2,1,0:T(8,128)(2,1)} %scatter_fusion), calls=%async_computation.2 | async-start | bytes 8388608 | tf_op jit(solution)/shard_map/all_to_all | solution.py:87
  49.7 47.6 %all-to-all-done.2 = bf16[256,64,128]{2,1,0:T(8,128)(2,1)} async-done(((bf16[256,64,128]{2,1,0:T(8,128)(2,1)}), bf16[256,64,128]{2,1,0:T(8,128)(2,1)}, u32[]{:S(2)}, u32[]{:S(2)}) %all-to-all-start.2) | async-done | bytes 4194336 | tf_op jit(solution)/shard_map/all_to_all | solution.py:87
  97.4 5.5 %all-to-all-start = ((s32[128,2,1]{1,2,0:T(1,128)}), s32[128,2,1]{1,2,0:T(1,128)S(1)}, u32[]{:S(2)}, u32[]{:S(2)}) async-start(s32[128,2,1]{1,2,0:T(1,128)} %bitcast.17), calls=%async_computation | async-start | bytes 131072 | tf_op jit(solution)/shard_map/all_to_all | solution.py:104
  123.1 97.7 %while.10 = (s32[]{:T(128)}, f32[4,64,64,128]{3,2,1,0:T(8,128)}, bf16[4,64,64,128]{3,2,1,0:T(8,128)(2,1)}, s32[4,64,4,128]{3,2,1,0:T(4,128)}, bf16[4,64,4,128]{3,2,1,0:T(4,128)(2,1)}, /*index=5*/s32[]{:T(128)}) while((s32[]{:T(128)}, f32[4,64,64,128]{3,2,1,0:T(8,128)}, bf16[4,64,64,128]{3,2,1,0:T(8,128)(2,1)}, s32[4,64,4,128]{3,2,1,0:T(4,128)}, ...), condition=%wide.region_9.10_spmd, body=%wide.region_8.9_spmd.sunk | while | flops 546832384 | bytes 37029488 | solution.py:67
  125.3 6.0 %fusion.82 = f32[64,64,128]{2,1,0:T(8,128)S(1)} fusion(s32[64,128]{1,0:T(8,128)S(1)} %get-tuple-element.123, bf16[64,128]{1,0:T(8,128)(2,1)S(1)} %get-tuple-element.124, bf16[4,64,64,128]{3,2,1,0:T(8,128)(2,1)} %get-tuple-element.145, s32[]{:T(128)} %get-tuple-element.137), kind=kOutput, calls=%fused_computation.15.clone.1 | convolution fusion | flops 136314880 | bytes 3195392 | tf_op jit(solution)/shard_map/while/body/eval_jaxpr/tfi,tij->tfj/dot_general | solution.py:54
  131.4 5.4 %fusion.83 = f32[64,64,128]{2,1,0:T(8,128)S(1)} fusion(s32[64,128]{1,0:T(8,128)S(1)} %get-tuple-element.125, bf16[64,128]{1,0:T(8,128)(2,1)S(1)} %get-tuple-element.126, bf16[4,64,64,128]{3,2,1,0:T(8,128)(2,1)S(1)} %copy-done, s32[]{:T(128)} %get-tuple-element.137), kind=kOutput, calls=%fused_computation.17.clone.1 | convolution fusion | flops 136314880 | bytes 3194884 | tf_op jit(solution)/shard_map/while/body/eval_jaxpr/tfi,tij->tfj/dot_general | solution.py:54
  136.8 5.4 %fusion.84 = f32[64,64,128]{2,1,0:T(8,128)S(1)} fusion(s32[64,128]{1,0:T(8,128)S(1)} %get-tuple-element.127, bf16[64,128]{1,0:T(8,128)(2,1)S(1)} %get-tuple-element.128, bf16[4,64,64,128]{3,2,1,0:T(8,128)(2,1)S(1)} %copy-done, s32[]{:T(128)} %get-tuple-element.137), kind=kOutput, calls=%fused_computation.16.clone.1 | convolution fusion | flops 136314880 | bytes 3194884 | tf_op jit(solution)/shard_map/while/body/eval_jaxpr/tfi,tij->tfj/dot_general | solution.py:54
  149.8 6.0 %fusion.82 = f32[64,64,128]{2,1,0:T(8,128)S(1)} fusion(s32[64,128]{1,0:T(8,128)S(1)} %get-tuple-element.123, bf16[64,128]{1,0:T(8,128)(2,1)S(1)} %get-tuple-element.124, bf16[4,64,64,128]{3,2,1,0:T(8,128)(2,1)} %get-tuple-element.145, s32[]{:T(128)} %get-tuple-element.137), kind=kOutput, calls=%fused_computation.15.clone.1 | convolution fusion | flops 136314880 | bytes 3195392 | tf_op jit(solution)/shard_map/while/body/eval_jaxpr/tfi,tij->tfj/dot_general | solution.py:54
  155.8 5.4 %fusion.83 = f32[64,64,128]{2,1,0:T(8,128)S(1)} fusion(s32[64,128]{1,0:T(8,128)S(1)} %get-tuple-element.125, bf16[64,128]{1,0:T(8,128)(2,1)S(1)} %get-tuple-element.126, bf16[4,64,64,128]{3,2,1,0:T(8,128)(2,1)S(1)} %copy-done, s32[]{:T(128)} %get-tuple-element.137), kind=kOutput, calls=%fused_computation.17.clone.1 | convolution fusion | flops 136314880 | bytes 3194884 | tf_op jit(solution)/shard_map/while/body/eval_jaxpr/tfi,tij->tfj/dot_general | solution.py:54
  161.2 5.4 %fusion.84 = f32[64,64,128]{2,1,0:T(8,128)S(1)} fusion(s32[64,128]{1,0:T(8,128)S(1)} %get-tuple-element.127, bf16[64,128]{1,0:T(8,128)(2,1)S(1)} %get-tuple-element.128, bf16[4,64,64,128]{3,2,1,0:T(8,128)(2,1)S(1)} %copy-done, s32[]{:T(128)} %get-tuple-element.137), kind=kOutput, calls=%fused_computation.16.clone.1 | convolution fusion | flops 136314880 | bytes 3194884 | tf_op jit(solution)/shard_map/while/body/eval_jaxpr/tfi,tij->tfj/dot_general | solution.py:54
  166.7 5.3 %bitcast_dynamic-update-slice_fusion.2 = f32[4,64,64,128]{3,2,1,0:T(8,128)} fusion(f32[4,64,64,128]{3,2,1,0:T(8,128)} %get-tuple-element.138, s32[]{:T(128)} %get-tuple-element.137, f32[64,64,128]{2,1,0:T(8,128)S(1)} %fusion.82, f32[64,64,128]{2,1,0:T(8,128)S(1)} %fusion.83, f32[64,64,128]{2,1,0:T(8,128)S(1)} %fusion.84, ...), kind=kOutput, calls=%fused_computation.18.clone.1 | convolution fusion | flops 137887744 | bytes 9487360 | tf_op jit(solution)/shard_map/while/body/eval_jaxpr/tfi,tij->tfj/dot_general | solution.py:54
  174.2 6.0 %fusion.82 = f32[64,64,128]{2,1,0:T(8,128)S(1)} fusion(s32[64,128]{1,0:T(8,128)S(1)} %get-tuple-element.123, bf16[64,128]{1,0:T(8,128)(2,1)S(1)} %get-tuple-element.124, bf16[4,64,64,128]{3,2,1,0:T(8,128)(2,1)} %get-tuple-element.145, s32[]{:T(128)} %get-tuple-element.137), kind=kOutput, calls=%fused_computation.15.clone.1 | convolution fusion | flops 136314880 | bytes 3195392 | tf_op jit(solution)/shard_map/while/body/eval_jaxpr/tfi,tij->tfj/dot_general | solution.py:54
  180.2 5.4 %fusion.83 = f32[64,64,128]{2,1,0:T(8,128)S(1)} fusion(s32[64,128]{1,0:T(8,128)S(1)} %get-tuple-element.125, bf16[64,128]{1,0:T(8,128)(2,1)S(1)} %get-tuple-element.126, bf16[4,64,64,128]{3,2,1,0:T(8,128)(2,1)S(1)} %copy-done, s32[]{:T(128)} %get-tuple-element.137), kind=kOutput, calls=%fused_computation.17.clone.1 | convolution fusion | flops 136314880 | bytes 3194884 | tf_op jit(solution)/shard_map/while/body/eval_jaxpr/tfi,tij->tfj/dot_general | solution.py:54
  185.7 5.4 %fusion.84 = f32[64,64,128]{2,1,0:T(8,128)S(1)} fusion(s32[64,128]{1,0:T(8,128)S(1)} %get-tuple-element.127, bf16[64,128]{1,0:T(8,128)(2,1)S(1)} %get-tuple-element.128, bf16[4,64,64,128]{3,2,1,0:T(8,128)(2,1)S(1)} %copy-done, s32[]{:T(128)} %get-tuple-element.137), kind=kOutput, calls=%fused_computation.16.clone.1 | convolution fusion | flops 136314880 | bytes 3194884 | tf_op jit(solution)/shard_map/while/body/eval_jaxpr/tfi,tij->tfj/dot_general | solution.py:54
  191.1 5.3 %bitcast_dynamic-update-slice_fusion.2 = f32[4,64,64,128]{3,2,1,0:T(8,128)} fusion(f32[4,64,64,128]{3,2,1,0:T(8,128)} %get-tuple-element.138, s32[]{:T(128)} %get-tuple-element.137, f32[64,64,128]{2,1,0:T(8,128)S(1)} %fusion.82, f32[64,64,128]{2,1,0:T(8,128)S(1)} %fusion.83, f32[64,64,128]{2,1,0:T(8,128)S(1)} %fusion.84, ...), kind=kOutput, calls=%fused_computation.18.clone.1 | convolution fusion | flops 137887744 | bytes 9487360 | tf_op jit(solution)/shard_map/while/body/eval_jaxpr/tfi,tij->tfj/dot_general | solution.py:54
  198.6 6.0 %fusion.82 = f32[64,64,128]{2,1,0:T(8,128)S(1)} fusion(s32[64,128]{1,0:T(8,128)S(1)} %get-tuple-element.123, bf16[64,128]{1,0:T(8,128)(2,1)S(1)} %get-tuple-element.124, bf16[4,64,64,128]{3,2,1,0:T(8,128)(2,1)} %get-tuple-element.145, s32[]{:T(128)} %get-tuple-element.137), kind=kOutput, calls=%fused_computation.15.clone.1 | convolution fusion | flops 136314880 | bytes 3195392 | tf_op jit(solution)/shard_map/while/body/eval_jaxpr/tfi,tij->tfj/dot_general | solution.py:54
  204.7 5.4 %fusion.83 = f32[64,64,128]{2,1,0:T(8,128)S(1)} fusion(s32[64,128]{1,0:T(8,128)S(1)} %get-tuple-element.125, bf16[64,128]{1,0:T(8,128)(2,1)S(1)} %get-tuple-element.126, bf16[4,64,64,128]{3,2,1,0:T(8,128)(2,1)S(1)} %copy-done, s32[]{:T(128)} %get-tuple-element.137), kind=kOutput, calls=%fused_computation.17.clone.1 | convolution fusion | flops 136314880 | bytes 3194884 | tf_op jit(solution)/shard_map/while/body/eval_jaxpr/tfi,tij->tfj/dot_general | solution.py:54
  210.1 5.4 %fusion.84 = f32[64,64,128]{2,1,0:T(8,128)S(1)} fusion(s32[64,128]{1,0:T(8,128)S(1)} %get-tuple-element.127, bf16[64,128]{1,0:T(8,128)(2,1)S(1)} %get-tuple-element.128, bf16[4,64,64,128]{3,2,1,0:T(8,128)(2,1)S(1)} %copy-done, s32[]{:T(128)} %get-tuple-element.137), kind=kOutput, calls=%fused_computation.16.clone.1 | convolution fusion | flops 136314880 | bytes 3194884 | tf_op jit(solution)/shard_map/while/body/eval_jaxpr/tfi,tij->tfj/dot_general | solution.py:54
  225.1 37.0 %scatter_fusion.1 = f32[256,64,128]{2,1,0:T(8,128)} fusion(f32[256,64,128]{2,1,0:T(8,128)} %broadcast_in_dim.116, s32[256]{0:T(256)S(1)} %compare_select_fusion.1, f32[256,64,128]{2,1,0:T(8,128)} %bitcast.25), kind=kCustom, calls=%fused_computation.5 | custom fusion | bytes 25166848 | tf_op jit(solution)/shard_map/scatter | solution.py:100
  262.1 10.3 %all-to-all-start.3 = ((f32[256,64,128]{2,1,0:T(8,128)}), f32[256,64,128]{2,1,0:T(8,128)}, u32[]{:S(2)}, u32[]{:S(2)}) async-start(f32[256,64,128]{2,1,0:T(8,128)} %scatter_fusion.1), calls=%async_computation.3 | async-start | bytes 16777216 | tf_op jit(solution)/shard_map/all_to_all | solution.py:103
  273.9 103.7 %all-to-all-done.3 = f32[256,64,128]{2,1,0:T(8,128)} async-done(((f32[256,64,128]{2,1,0:T(8,128)}), f32[256,64,128]{2,1,0:T(8,128)}, u32[]{:S(2)}, u32[]{:S(2)}) %all-to-all-start.3) | async-done | bytes 8388640 | tf_op jit(solution)/shard_map/all_to_all | solution.py:103
  377.7 10.4 %fusion.42 = f32[4,64,128]{2,0,1:T(4,128)S(1)} fusion(f32[256,64,128]{2,1,0:T(8,128)} %all-to-all-done.3, s32[256]{0:T(256)S(1)} %eq.127), kind=kOutput, calls=%fused_computation.59 | convolution fusion | flops 100664320 | bytes 8520704 | tf_op jit(solution)/shard_map/ot,tfj->ofj/dot_general | solution.py:109
  (92 shorter events, 57.9 us)
Async XLA Ops:
  0.0 19.4 %copy-start.1 = (bf16[128,64,128]{2,1,0:T(8,128)(2,1)S(1)}, bf16[128,64,128]{2,1,0:T(8,128)(2,1)}, u32[]{:S(2)}) copy-start(bf16[128,64,128]{2,1,0:T(8,128)(2,1)} %param.12) | copy-start | bytes 6291460
  4.8 30.2 %all-to-all-start.1 = ((s32[128,2,5]{2,1,0:T(2,128)}), s32[128,2,5]{2,1,0:T(2,128)S(1)}, u32[]{:S(2)}, u32[]{:S(2)}) async-start(s32[128,2,5]{2,1,0:T(2,128)} %bitcast.19), calls=%async_computation.1 | async-start | bytes 262144 | tf_op jit(solution)/shard_map/all_to_all | solution.py:88
  35.1 10.3 %copy-start.3 = (s32[256]{0:T(256)S(1)}, s32[256]{0:T(256)}, u32[]{:S(2)}) copy-start(s32[256]{0:T(256)} %param.15) | copy-start | bytes 3076
  35.1 10.4 %copy-start.2 = (s32[256]{0:T(256)S(1)}, s32[256]{0:T(256)}, u32[]{:S(2)}) copy-start(s32[256]{0:T(256)} %param.16) | copy-start | bytes 3076
  35.1 13.5 %copy-start.5 = (s32[128]{0:T(128)S(1)}, s32[128]{0:T(128)}, u32[]{:S(2)}) copy-start(s32[128]{0:T(128)} %constant.103) | copy-start | bytes 1540
  35.1 14.4 %copy-start.4 = (s32[128]{0:T(128)S(1)}, s32[128]{0:T(128)}, u32[]{:S(2)}) copy-start(s32[128]{0:T(128)} %constant.101.clone) | copy-start | bytes 1540
  35.1 62.3 %all-to-all-start.2 = ((bf16[256,64,128]{2,1,0:T(8,128)(2,1)}), bf16[256,64,128]{2,1,0:T(8,128)(2,1)}, u32[]{:S(2)}, u32[]{:S(2)}) async-start(bf16[256,64,128]{2,1,0:T(8,128)(2,1)} %scatter_fusion), calls=%async_computation.2 | async-start | bytes 8388608 | tf_op jit(solution)/shard_map/all_to_all | solution.py:87
  97.4 164.8 %all-to-all-start = ((s32[128,2,1]{1,2,0:T(1,128)}), s32[128,2,1]{1,2,0:T(1,128)S(1)}, u32[]{:S(2)}, u32[]{:S(2)}) async-start(s32[128,2,1]{1,2,0:T(1,128)} %bitcast.17), calls=%async_computation | async-start | bytes 131072 | tf_op jit(solution)/shard_map/all_to_all | solution.py:104
  123.1 8.3 %copy-start = (bf16[4,64,64,128]{3,2,1,0:T(8,128)(2,1)S(1)}, bf16[4,64,64,128]{3,2,1,0:T(8,128)(2,1)}, u32[]{:S(2)}) copy-start(bf16[4,64,64,128]{3,2,1,0:T(8,128)(2,1)} %get-tuple-element.145) | copy-start | bytes 12582916 | tf_op jit(solution)/shard_map/while
  147.5 8.3 %copy-start = (bf16[4,64,64,128]{3,2,1,0:T(8,128)(2,1)S(1)}, bf16[4,64,64,128]{3,2,1,0:T(8,128)(2,1)}, u32[]{:S(2)}) copy-start(bf16[4,64,64,128]{3,2,1,0:T(8,128)(2,1)} %get-tuple-element.145) | copy-start | bytes 12582916 | tf_op jit(solution)/shard_map/while
  172.0 8.3 %copy-start = (bf16[4,64,64,128]{3,2,1,0:T(8,128)(2,1)S(1)}, bf16[4,64,64,128]{3,2,1,0:T(8,128)(2,1)}, u32[]{:S(2)}) copy-start(bf16[4,64,64,128]{3,2,1,0:T(8,128)(2,1)} %get-tuple-element.145) | copy-start | bytes 12582916 | tf_op jit(solution)/shard_map/while
  196.4 8.3 %copy-start = (bf16[4,64,64,128]{3,2,1,0:T(8,128)(2,1)S(1)}, bf16[4,64,64,128]{3,2,1,0:T(8,128)(2,1)}, u32[]{:S(2)}) copy-start(bf16[4,64,64,128]{3,2,1,0:T(8,128)(2,1)} %get-tuple-element.145) | copy-start | bytes 12582916 | tf_op jit(solution)/shard_map/while
  262.1 115.5 %all-to-all-start.3 = ((f32[256,64,128]{2,1,0:T(8,128)}), f32[256,64,128]{2,1,0:T(8,128)}, u32[]{:S(2)}, u32[]{:S(2)}) async-start(f32[256,64,128]{2,1,0:T(8,128)} %scatter_fusion.1), calls=%async_computation.3 | async-start | bytes 16777216 | tf_op jit(solution)/shard_map/all_to_all | solution.py:103
where the time goes:
time: 394 us; the launch traced here: 389 us
  waiting for transfers between devices  151 us (38%)
  matrix products  99.1 us (25%)
  local copies, waits for them, and re-layouts  87.5 us (22%)
  starting transfers between devices  37.6 us (10%)
  other arithmetic  12.6 us (3%)
    all_to_all x1, waiting for transfers between devices, on_device(): lax.all_to_all(partial_out, ('comp', 'cpl'), split_axis=0, concat_axis=0,...  104 us
    dot_general x16, matrix products, remap_group(): jnp.einsum('tfi,tij->tfj', block_rows, dense, preferred_element_type=jnp....  88.7 us
    all_to_all x1, waiting for transfers between devices, on_device(): lax.all_to_all(outgoing, ('comp', 'cpl'), split_axis=0, concat_axis=0, ti...  47.6 us
    scatter x1, local copies, waits for them, and re-layouts, on_device(): jnp.zeros(partial_value.shape, jnp.float32).at[send_at]  37 us
    scatter x1, local copies, waits for them, and re-layouts, on_device(): jnp.zeros((slot_total, field_count, block_cols), jnp.bfloat16).at[home_slot]  15.7 us
    all_to_all x1, starting transfers between devices, on_device(): lax.all_to_all(packed_out, ('comp', 'cpl'), split_axis=0, concat_axis=0,...  11.5 us
    dot_general x1, matrix products, on_device(): jnp.einsum('ot,tfj->ofj', selector, arrived, precision=lax.Precision.HIGH...  10.4 us
    all_to_all x1, starting transfers between devices, on_device(): lax.all_to_all(partial_out, ('comp', 'cpl'), split_axis=0, concat_axis=0,...  10.3 us
  transfers between devices with their start and end apart: 4, of which 2 were waited for; matrix products, arithmetic and copies ran while one was open for 47% of the time, Pallas kernels for 0%

commit v1 on v0

v1 whole, which is shorter than its diff:
```python
import jax
import jax.numpy as jnp
from jax import lax
from jax.experimental import pallas as pl
from jax.experimental.pallas import tpu as pltpu
from jax.sharding import PartitionSpec as P

AXES = ("comp", "cpl")
ENTRIES = 4
CHUNK = 5
VMEM_LIMIT = 24 * 1024 * 1024


def pack_kernel(ranks, ocean_blocks, col_ref, row_ref, weight_ref, target_ref, out_ref, slot_row):
    tiles = weight_ref.shape[0]
    block = weight_ref.shape[2]

    def place(t, carry):
        slot = col_ref[t]
        slot_row[slot] = row_ref[t]
        base = (slot >> 1) * CHUNK + (slot & 1) * 2
        out_ref[base] = weight_ref[t]
        out_ref[base + 1] = target_ref[t].astype(jnp.float32).astype(jnp.bfloat16)
        return carry

    lax.fori_loop(0, tiles, place, 0, unroll=8)

    lane = lax.broadcasted_iota(jnp.int32, (1, block), 1)

    def destination(s, found):
        best = jnp.maximum(slot_row[2 * s], slot_row[2 * s + 1])
        device = jnp.where(best >= 0, best // ocean_blocks + 1, 0)
        return jnp.where(lane == s, device, found)

    found = lax.fori_loop(0, ranks, destination, jnp.zeros((1, block), jnp.int32), unroll=8)
    entry = lax.broadcasted_iota(jnp.int32, (ENTRIES, block), 0)
    found = jnp.where(entry == 2, jnp.broadcast_to(found, (ENTRIES, block)), 0)

    def rows_of(s, carry):
        first = slot_row[2 * s]
        second = slot_row[2 * s + 1]
        first = jnp.where(first >= 0, first % ocean_blocks + 1, 0)
        second = jnp.where(second >= 0, second % ocean_blocks + 1, 0)
        rows = jnp.where(entry == 0, first, jnp.where(entry == 1, second, found))
        out_ref[s * CHUNK + 4] = rows.astype(jnp.float32).astype(jnp.bfloat16)
        return carry

    lax.fori_loop(0, ranks, rows_of, 0, unroll=8)


def flux_kernel(owner_ref, bits_ref, atm_ref, sent_ref, out_ref, slot_ref, ocean_ref, count_ref):
    blocks, _, block = atm_ref.shape

    def clear(c, carry):
        count_ref[c] = 0
        return carry

    lax.fori_loop(0, count_ref.shape[0], clear, 0, unroll=8)

    def home(b, carry):
        owner = owner_ref[b]
        rank = count_ref[owner]
        count_ref[owner] = rank + 1
        slot_ref[b] = 2 * owner + rank
        return carry

    lax.fori_loop(0, blocks, home, 0, unroll=4)

    column = lax.broadcasted_iota(jnp.int32, (blocks, block), 1)
    word = column // 30
    bits = bits_ref[...]
    picked = jnp.zeros((blocks, block), jnp.int32)
    for w in range(bits.shape[1]):
        picked = jnp.where(word == w, jnp.broadcast_to(bits[:, w : w + 1], (blocks, block)), picked)
    ocean_ref[...] = jnp.right_shift(picked, column - word * 30) & 1

    field = lax.broadcasted_iota(jnp.int32, (8, block), 0)

    def one_block(b, carry):
        state = atm_ref[b, 0:16, :].astype(jnp.float32)
        head = state[0:8]
        wind_east = head[0:1]
        wind_north = head[1:2]
        speed = jnp.sqrt(wind_east * wind_east + wind_north * wind_north + 0.25)
        later = pltpu.roll(head, 6, 0)
        drive = jnp.where(field < 2, head, later - head)
        bulk = (0.5 * speed) * drive
        ocean = jnp.broadcast_to(ocean_ref[pl.ds(b, 1), :], (8, block))
        head = jnp.where((ocean == 1) & (field < 4), bulk, head)
        out_ref[b, 0:16, :] = jnp.concatenate([head, state[8:16]], 0).astype(jnp.bfloat16)
        out_ref[b, 16:64, :] = atm_ref[b, 16:64, :]
        return carry

    lax.fori_loop(0, blocks, one_block, 0, unroll=4)


def remap_kernel(slot_ref, recv_ref, flux_ref, out_ref, owner_ref, rows_vmem, rows_smem, sem):
    blocks, _, block = flux_ref.shape
    ranks = recv_ref.shape[0] // CHUNK
    entry = lax.broadcasted_iota(jnp.int32, (ENTRIES, block), 0)
    lane = lax.broadcasted_iota(jnp.int32, (ENTRIES, block), 1)

    def gather_rows(c, found):
        rows = recv_ref[c * CHUNK + 4].astype(jnp.float32)
        return jnp.maximum(found, jnp.where((lane == c) | (entry == 2), rows, 0.0))

    found = lax.fori_loop(0, ranks, gather_rows, jnp.zeros((ENTRIES, block), jnp.float32), unroll=8)
    found = jnp.concatenate([found, jnp.zeros((ENTRIES, block), jnp.float32)], 0)
    owner_ref[...] = found
    rows_vmem[...] = found.astype(jnp.int32)
    copy = pltpu.make_async_copy(rows_vmem, rows_smem, sem)
    copy.start()
    out_ref[...] = jnp.zeros_like(out_ref)
    copy.wait()

    column = lax.broadcasted_iota(jnp.int32, (block, block), 0).astype(jnp.float32).astype(jnp.bfloat16)

    def one_tile(b, carry):
        slot = slot_ref[b]
        source = slot >> 1
        rank = slot & 1
        base = source * CHUNK + rank * 2
        row = rows_smem[rank, source] - 1
        weight = recv_ref[base]
        target = recv_ref[base + 1]
        dense = [
            jnp.where(
                jnp.broadcast_to(target[k : k + 1], (block, block)) == column,
                jnp.broadcast_to(weight[k : k + 1], (block, block)),
                jnp.zeros((), jnp.bfloat16),
            )
            for k in range(ENTRIES)
        ]
        fluxes = flux_ref[b]
        out_ref[row] += lax.dot_general(
            jnp.concatenate([fluxes] * ENTRIES, 1),
            jnp.concatenate(dense, 1),
            (((1,), (1,)), ((), ())),
            preferred_element_type=jnp.float32,
        )
        return carry

    lax.fori_loop(0, blocks, one_tile, 0, unroll=4)


def permute_kernel(owner_ref, x_ref, out_ref):
    ranks, pieces, block = x_ref.shape
    rows = ranks * pieces
    source = lax.broadcasted_iota(jnp.int32, (block, rows), 0)
    spread = (lax.broadcasted_iota(jnp.int32, (block, rows), 1) // pieces == source)
    owner = jnp.dot(
        owner_ref[...].astype(jnp.bfloat16),
        spread.astype(jnp.float32).astype(jnp.bfloat16),
        preferred_element_type=jnp.float32,
    )[2:3]
    half = lax.broadcasted_iota(jnp.int32, (1, rows), 1) % pieces
    wanted = (owner.astype(jnp.int32) - 1) * pieces + half
    chosen = lax.broadcasted_iota(jnp.int32, (rows, rows), 0) == jnp.broadcast_to(wanted, (rows, rows))
    chosen = chosen.astype(jnp.float32).astype(jnp.bfloat16)
    value = x_ref[...].reshape(rows, block)
    high = value.astype(jnp.bfloat16)
    rest = value - high.astype(jnp.float32)
    middle = rest.astype(jnp.bfloat16)
    low = (rest - middle.astype(jnp.float32)).astype(jnp.bfloat16)
    total = jnp.dot(chosen, high, preferred_element_type=jnp.float32)
    total += jnp.dot(chosen, middle, preferred_element_type=jnp.float32)
    total += jnp.dot(chosen, low, preferred_element_type=jnp.float32)
    out_ref[...] = total.reshape(ranks, pieces, block)


def smem():
    return pl.BlockSpec(memory_space=pltpu.SMEM)


def vmem():
    return pl.BlockSpec(memory_space=pltpu.VMEM)


def exchange(x):
    return lax.all_to_all(x, AXES, split_axis=0, concat_axis=0, tiled=True)


def on_device(atm_fields, land_bits, coupler_owner, tile_col, tile_row, tile_weight, tile_target):
    ranks = lax.axis_size("comp") * lax.axis_size("cpl")
    blocks, fields, block = atm_fields.shape
    ocean_blocks = blocks // 32
    params = pltpu.CompilerParams(vmem_limit_bytes=VMEM_LIMIT)

    send = pl.pallas_call(
        lambda *refs: pack_kernel(ranks, ocean_blocks, *refs),
        out_shape=jax.ShapeDtypeStruct((ranks * CHUNK, ENTRIES, block), jnp.bfloat16),
        in_specs=[smem(), smem(), vmem(), vmem()],
        out_specs=vmem(),
        scratch_shapes=[pltpu.SMEM((tile_col.shape[0],), jnp.int32)],
        compiler_params=params,
        name="pack",
    )(tile_col, tile_row, tile_weight, tile_target)
    recv = exchange(send)

    fluxes, slot = pl.pallas_call(
        flux_kernel,
        out_shape=(
            jax.ShapeDtypeStruct(atm_fields.shape, jnp.bfloat16),
            jax.ShapeDtypeStruct((blocks,), jnp.int32),
        ),
        in_specs=[smem(), vmem(), vmem(), pl.BlockSpec(memory_space=pl.ANY)],
        out_specs=(vmem(), smem()),
        scratch_shapes=[pltpu.VMEM((blocks, block), jnp.int32), pltpu.SMEM((ranks,), jnp.int32)],
        compiler_params=params,
        cost_estimate=pl.CostEstimate(flops=10_000_000, bytes_accessed=4_000_000, transcendentals=0),
        name="flux",
    )(coupler_owner, land_bits, atm_fields, send)

    sums, owner = pl.pallas_call(
        remap_kernel,
        out_shape=(
            jax.ShapeDtypeStruct((ocean_blocks, fields, block), jnp.float32),
            jax.ShapeDtypeStruct((8, block), jnp.float32),
        ),
        in_specs=[smem(), vmem(), vmem()],
        out_specs=(vmem(), vmem()),
        scratch_shapes=[
            pltpu.VMEM((8, block), jnp.int32),
            pltpu.SMEM((8, block), jnp.int32),
            pltpu.SemaphoreType.DMA,
        ],
        compiler_params=params,
        name="remap",
    )(slot, recv, fluxes)

    pieces = ocean_blocks * fields // ranks
    spread = exchange(sums.reshape(ranks, pieces, block))
    turned = pl.pallas_call(
        permute_kernel,
        out_shape=jax.ShapeDtypeStruct(spread.shape, jnp.float32),
        in_specs=[vmem(), vmem()],
        out_specs=vmem(),
        compiler_params=params,
        name="permute",
    )(owner, spread)
    return exchange(turned).reshape(ocean_blocks, fields, block)


def solution(mesh):
    in_specs = (
        P(AXES, None, None),
        P(AXES, None),
        P(AXES),
        P(AXES),
        P(AXES),
        P(AXES, None, None),
        P(AXES, None, None),
    )
    return jax.shard_map(
        on_device, mesh=mesh, in_specs=in_specs, out_specs=P(AXES, None, None), check_vma=False
    )
```

time: 394 us -> 76.7 us (0.19); the launches traced: 389 us -> 76.4 us
  waiting for transfers between devices: 151 us -> 10.8 us
  matrix products: 99.1 us -> 0 us
  local copies, waits for them, and re-layouts: 87.5 us -> 7.19 us
  blocking collectives: 0 us -> 28.3 us
  starting transfers between devices: 37.6 us -> 11.5 us
  Pallas kernels: 0 us -> 18.5 us
  other arithmetic: 12.6 us -> 0 us
    all_to_all x4 -> x1, waiting for transfers between devices: 151 us -> 10.8 us  [exchange(): return lax.all_to_all(x, AXES, split_axis=0, concat_axis=0, tiled=True)]
    dot_general x17 -> x0, matrix products: 99.1 us -> none  [the longest x16 88.7 us: remap_group(): jnp.einsum('tfi,tij->tfj', block_rows, dense, preferred_element_type=jnp....]
    scatter x4 -> x0, local copies, waits for them, and re-layouts: 55.6 us -> none  [the longest x1 37 us: on_device(): jnp.zeros(partial_value.shape, jnp.float32).at[send_at]]
    all_to_all x0 -> x2, blocking collectives: none -> 28.3 us  [exchange(): return lax.all_to_all(x, AXES, split_axis=0, concat_axis=0, tiled=True)]
    all_to_all x4 -> x1, starting transfers between devices: 37.6 us -> 11.5 us  [exchange(): return lax.all_to_all(x, AXES, split_axis=0, concat_axis=0, tiled=True)]
    pallas_call x0 -> x4, Pallas kernels: none -> 18.5 us  [the longest x1 11 us: on_device(): pl.pallas_call(remap_kernel, out_shape=(jax.ShapeDtypeStruct((ocean_block...]
    dynamic_slice x16 -> x0, local copies, waits for them, and re-layouts: 8.66 us -> none  [remap_tiles(): result = lax.map(remap_group, shaped)]
    broadcast_in_dim x7 -> x0, local copies, waits for them, and re-layouts: 7.41 us -> none  [the longest x1 4.28 us: on_device(): jnp.zeros(partial_value.shape, jnp.float32).at[send_at]]
  transfers between devices with their start and end apart: 4 -> 1, of which waited for: 2 -> 1; matrix products, arithmetic and copies ran while one was open for 47% -> 0% of each run, Pallas kernels for 0% -> 4%
where the time goes in v1:
time: 76.7 us; the launch traced here: 76.4 us
  blocking collectives  28.3 us (37%)
  Pallas kernels  18.5 us (24%)
  starting transfers between devices  11.5 us (15%)
  waiting for transfers between devices  10.8 us (14%)
  local copies, waits for them, and re-layouts  7.19 us (9%)
    all_to_all x2, blocking collectives, exchange(): return lax.all_to_all(x, AXES, split_axis=0, concat_axis=0, tiled=True)  28.3 us
    all_to_all x1, starting transfers between devices, exchange(): return lax.all_to_all(x, AXES, split_axis=0, concat_axis=0, tiled=True)  11.5 us
    pallas_call x1, Pallas kernels, on_device(): pl.pallas_call(remap_kernel, out_shape=(jax.ShapeDtypeStruct((ocean_block...  11 us
    all_to_all x1, waiting for transfers between devices, exchange(): return lax.all_to_all(x, AXES, split_axis=0, concat_axis=0, tiled=True)  10.8 us
    unnamed x20, local copies, waits for them, and re-layouts  7.19 us
    pallas_call x1, Pallas kernels, on_device(): pl.pallas_call(lambda *refs: pack_kernel(ranks, ocean_blocks, *refs), out...  4.29 us
    pallas_call x1, Pallas kernels, on_device(): pl.pallas_call(flux_kernel, out_shape=(jax.ShapeDtypeStruct(atm_fields.sh...  2.87 us
  transfers between devices with their start and end apart: 1, of which 1 were waited for; matrix products, arithmetic and copies ran while one was open for 0% of the time, Pallas kernels for 4%

profile of v1, /device:TPU:1, one launch (start us, length us, event | category | flops | bytes accessed | tf_op | source)
XLA Modules:
  0.0 76.4 jit_solution(10851010969379546845)
XLA Ops:
  0.0 0.0 copy-start
  0.0 0.0 copy-start.3
  0.0 1.2 %copy-done.3 = s32[256,4,128]{2,1,0:T(4,128)S(1)} copy-done((s32[256,4,128]{2,1,0:T(4,128)S(1)}, s32[256,4,128]{2,1,0:T(4,128)}, u32[]{:S(2)}) %copy-start.3) | copy-done | bytes 524312
  1.2 0.9 %copy-done.4 = bf16[256,4,128]{2,1,0:T(4,128)(2,1)S(1)} copy-done((bf16[256,4,128]{2,1,0:T(4,128)(2,1)S(1)}, bf16[256,4,128]{2,1,0:T(4,128)(2,1)}, u32[]{:S(2)}) %copy-start.4) | copy-done | bytes 262168
  2.1 0.0 copy-start.5
  2.1 0.7 copy-done.5
  2.8 0.7 copy-done.6
  3.5 0.0 copy-start.8
  3.5 4.3 %pack.1.sent_ref = bf16[640,4,128]{2,1,0:T(4,128)(2,1)} custom-call(s32[256]{0:T(256)S(1)} %copy-done.5, s32[256]{0:T(256)S(1)} %copy-done.6, bf16[256,4,128]{2,1,0:T(4,128)(2,1)S(1)} %copy-done.4, s32[256,4,128]{2,1,0:T(4,128)S(1)} %copy-done.3), custom_call_target="tpu_custom_call" | custom-call | tf_op jit(solution)/shard_map/pack/pallas_call | solution.py:189
  7.8 11.5 %all-to-all-start = ((bf16[640,4,128]{2,1,0:T(4,128)(2,1)}), bf16[640,4,128]{2,1,0:T(4,128)(2,1)S(1)}, u32[]{:S(2)}, u32[]{:S(2)}) async-start(bf16[640,4,128]{2,1,0:T(4,128)(2,1)} %pack.1.sent_ref), calls=%async_computation | async-start | bytes 1310720 | tf_op jit(solution)/shard_map/all_to_all | solution.py:180
  19.3 0.0 copy-done.8
  19.3 0.1 copy.8.bits_ref
  19.4 0.0 copy-done
  19.4 0.0 copy-done.7
  19.4 2.9 %flux.1 = (bf16[128,64,128]{2,1,0:T(8,128)(2,1)S(1)}, s32[128]{0:T(128)S(1)}) custom-call(s32[128]{0:T(128)S(1)} %copy-done.7, s32[128,5]{1,0:T(8,128)S(1)} %copy.8.bits_ref, bf16[128,64,128]{2,1,0:T(8,128)(2,1)S(1)} %copy-done, bf16[640,4,128]{2,1,0:T(4,128)(2,1)} %pack.1.sent_ref), custom_call_target="tpu_custom_call" | custom-call | flops 10000000 | bytes 4000000 | tf_op jit(solution)/shard_map/flux/pallas_call | solution.py:200
  22.3 0.0 copy-start.1
  22.3 1.3 %copy-done.1 = bf16[128,64,128]{2,1,0:T(8,128)(2,1)} copy-done((bf16[128,64,128]{2,1,0:T(8,128)(2,1)}, bf16[128,64,128]{2,1,0:T(8,128)(2,1)S(1)}, u32[]{:S(2)}) %copy-start.1) | copy-done | bytes 2097176
  23.6 10.8 %all-to-all-done.recv_ref = bf16[640,4,128]{2,1,0:T(4,128)(2,1)S(1)} async-done(((bf16[640,4,128]{2,1,0:T(4,128)(2,1)}), bf16[640,4,128]{2,1,0:T(4,128)(2,1)S(1)}, u32[]{:S(2)}, u32[]{:S(2)}) %all-to-all-start) | async-done | bytes 655392 | tf_op jit(solution)/shard_map/all_to_all | solution.py:180
  34.5 1.6 %copy-done.2 = bf16[128,64,128]{2,1,0:T(8,128)(2,1)S(1)} copy-done((bf16[128,64,128]{2,1,0:T(8,128)(2,1)S(1)}, bf16[128,64,128]{2,1,0:T(8,128)(2,1)}, u32[]{:S(2)}) %copy-start.2) | copy-done | bytes 2097176
  36.1 11.0 %remap.1 = (f32[4,64,128]{2,1,0:T(8,128)S(1)}, f32[8,128]{1,0:T(8,128)S(1)}) custom-call(s32[128]{0:T(128)S(1)} %get-tuple-element.9.slot_ref, bf16[640,4,128]{2,1,0:T(4,128)(2,1)S(1)} %all-to-all-done.recv_ref, bf16[128,64,128]{2,1,0:T(8,128)(2,1)S(1)} %copy-done.2), custom_call_target="tpu_custom_call" | custom-call | tf_op jit(solution)/shard_map/remap/pallas_call | solution.py:214
  47.1 14.1 %all_to_all.15.x_ref = f32[128,2,128]{2,1,0:T(2,128)S(1)} all-to-all(f32[128,2,128]{2,1,0:T(2,128)S(1)} %bitcast.2), channel_id=1, replica_groups=mesh['comp'=8,'cpl'=16] {'comp','cpl'}, dimensions={0} | all-to-all | bytes 262144 | tf_op jit(solution)/shard_map/all_to_all | solution.py:180
  61.2 0.4 permute.1
  61.6 14.2 %all_to_all.16 = f32[128,2,128]{2,1,0:T(2,128)S(1)} all-to-all(f32[128,2,128]{2,1,0:T(2,128)S(1)} %permute.1), channel_id=1, replica_groups=mesh['comp'=8,'cpl'=16] {'comp','cpl'}, dimensions={0} | all-to-all | bytes 262144 | tf_op jit(solution)/shard_map/all_to_all | solution.py:180
  75.8 0.7 copy.10
  (4 shorter events, 0.0 us)
Async XLA Ops:
  0.0 19.4 %copy-start = (bf16[128,64,128]{2,1,0:T(8,128)(2,1)S(1)}, bf16[128,64,128]{2,1,0:T(8,128)(2,1)}, u32[]{:S(2)}) copy-start(bf16[128,64,128]{2,1,0:T(8,128)(2,1)} %atm_ref.1) | copy-start | bytes 6291460
  0.0 1.2 %copy-start.3 = (s32[256,4,128]{2,1,0:T(4,128)S(1)}, s32[256,4,128]{2,1,0:T(4,128)}, u32[]{:S(2)}) copy-start(s32[256,4,128]{2,1,0:T(4,128)} %refs_3_.1) | copy-start | bytes 1572868
  1.2 0.9 %copy-start.4 = (bf16[256,4,128]{2,1,0:T(4,128)(2,1)S(1)}, bf16[256,4,128]{2,1,0:T(4,128)(2,1)}, u32[]{:S(2)}) copy-start(bf16[256,4,128]{2,1,0:T(4,128)(2,1)} %refs_2_.1) | copy-start | bytes 786436
  2.1 0.7 copy-start.5
  2.8 0.7 copy-start.6
  3.5 15.8 %copy-start.8 = (s32[128,5]{0,1:T(8,128)S(1)}, s32[128,5]{0,1:T(8,128)}, u32[]{:S(2)}) copy-start(s32[128,5]{0,1:T(8,128)} %param.8) | copy-start | bytes 7684
  3.5 15.9 %copy-start.7 = (s32[128]{0:T(128)S(1)}, s32[128]{0:T(128)}, u32[]{:S(2)}) copy-start(s32[128]{0:T(128)} %owner_ref.1) | copy-start | bytes 1540
  7.8 26.7 %all-to-all-start = ((bf16[640,4,128]{2,1,0:T(4,128)(2,1)}), bf16[640,4,128]{2,1,0:T(4,128)(2,1)S(1)}, u32[]{:S(2)}, u32[]{:S(2)}) async-start(bf16[640,4,128]{2,1,0:T(4,128)(2,1)} %pack.1.sent_ref), calls=%async_computation | async-start | bytes 1310720 | tf_op jit(solution)/shard_map/all_to_all | solution.py:180
  22.3 1.3 %copy-start.1 = (bf16[128,64,128]{2,1,0:T(8,128)(2,1)}, bf16[128,64,128]{2,1,0:T(8,128)(2,1)S(1)}, u32[]{:S(2)}) copy-start(bf16[128,64,128]{2,1,0:T(8,128)(2,1)S(1)} %get-tuple-element.10.flux_ref) | copy-start | bytes 6291460
  34.5 1.6 %copy-start.2 = (bf16[128,64,128]{2,1,0:T(8,128)(2,1)S(1)}, bf16[128,64,128]{2,1,0:T(8,128)(2,1)}, u32[]{:S(2)}) copy-start(bf16[128,64,128]{2,1,0:T(8,128)(2,1)} %copy-done.1) | copy-start | bytes 6291460

commit v2 on v1

v2 whole, which is shorter than its diff:
```python
import jax
import jax.numpy as jnp
from jax import lax
from jax.experimental import pallas as pl
from jax.experimental.pallas import tpu as pltpu
from jax.sharding import PartitionSpec as P

AXES = ("comp", "cpl")
ENTRIES = 4
RATIO = 32
CHUNK = 5
VMEM_LIMIT = 24 * 1024 * 1024
BF16 = jnp.bfloat16
F32 = jnp.float32
I32 = jnp.int32
ROWS_WITH_ROWS = (((1,), (1,)), ((), ()))


def start_copies(pairs, sems):
    copies = [pltpu.make_async_copy(a, b, sems.at[i]) for i, (a, b) in enumerate(pairs)]
    for copy in copies:
        copy.start()
    return copies


def regroup(target, weight):
    t0, t1, t2, t3 = target
    w0, w1, w2, w3 = weight
    e01, e02, e03 = t0 == t1, t0 == t2, t0 == t3
    e12, e13, e23 = t1 == t2, t1 == t3, t2 == t3
    zero = jnp.zeros_like(w0)
    swap = e01 | e23
    a1t, a1w = jnp.where(swap, t2, t1), jnp.where(swap, w2, w1)
    b0t, b0w = jnp.where(swap, t1, t2), jnp.where(swap, w1, w2)
    with_first = (e01 & e02) | (e01 & e03) | (e02 & e03)
    rest = e12 & e13 & jnp.logical_not(with_first)
    sum0 = w0 + jnp.where(e01, w1, zero) + jnp.where(e02, w2, zero) + jnp.where(e03, w3, zero)
    sum1 = w1 + w2 + w3
    high0 = sum0.astype(BF16).astype(F32)
    high1 = sum1.astype(BF16).astype(F32)
    other_t = jnp.where(e01, jnp.where(e02, t3, t2), t1)
    other_w = jnp.where(e01, jnp.where(e02, w3, w2), w1)
    a0w = jnp.where(with_first, high0, w0)
    a1t = jnp.where(with_first, other_t, jnp.where(rest, t1, a1t))
    a1w = jnp.where(with_first, other_w, jnp.where(rest, high1, a1w))
    b0t = jnp.where(with_first, t0, jnp.where(rest, t1, b0t))
    b0w = jnp.where(with_first, sum0 - high0, jnp.where(rest, sum1 - high1, b0w))
    b1t = jnp.where(with_first, t0, jnp.where(rest, t1, t3))
    b1w = jnp.where(with_first | rest, b0w, w3)
    return (t0, a1t, b0t, b1t), (a0w, a1w, b0w, b1w)


def pack_kernel(
    ranks, ocean_blocks, col_hbm, col2_hbm, row2_hbm, weight_hbm, target_hbm,
    out_ref, col, col2, row2, weight_in, target_in, weight, target, sems,
):
    tiles = col.shape[0]
    block = weight.shape[1]
    halves = tiles // block
    copies = start_copies(
        ((col2_hbm, col2), (row2_hbm, row2), (col_hbm, col), (weight_hbm, weight_in), (target_hbm, target_in)), sems
    )

    copies[0].wait()
    copies[1].wait()
    slot = (col2[...] & 1) * ranks + (col2[...] >> 1)
    entry = lax.broadcasted_iota(I32, (8, block), 0)
    place = lax.broadcasted_iota(I32, (tiles, block), 0)
    onehot, values = [], []
    for h in range(halves):
        same = jnp.broadcast_to(slot[h : h + 1], (tiles, block)) == place
        onehot.append(jnp.where(same, 1.0, 0.0).astype(BF16))
        row = jnp.broadcast_to(row2[h : h + 1], (8, block))
        device = jnp.where(row >= 0, row // ocean_blocks + 1, 0)
        local = jnp.where(row >= 0, row % ocean_blocks, 0)
        values.append(jnp.where(entry == 0, local, device).astype(F32).astype(BF16))
    found = lax.dot_general(
        jnp.concatenate(values, 1), jnp.concatenate(onehot, 1), ROWS_WITH_ROWS, preferred_element_type=F32
    )
    entry = entry[:ENTRIES]
    local0 = jnp.broadcast_to(found[0:1, :ranks], (ENTRIES, block))
    local1 = jnp.broadcast_to(found[0:1, ranks:], (ENTRIES, block))
    device = jnp.broadcast_to(jnp.maximum(found[1:2, :ranks], found[1:2, ranks:]), (ENTRIES, block))
    info = jnp.where(entry == 0, local0, jnp.where(entry == 1, local1, device)).astype(BF16)

    def tell(s, carry):
        out_ref[s * CHUNK + 4] = info
        return carry

    lax.fori_loop(0, ranks, tell, 0, unroll=16)

    copies[3].wait()

    def widen(g, carry):
        at = pl.ds(pl.multiple_of(g * 16, 16), 16)
        weight[at] = weight_in[at].astype(F32)
        return carry

    lax.fori_loop(0, weight.shape[0] // 16, widen, 0, unroll=8)
    copies[4].wait()

    def pair_up(g, carry):
        base = pl.multiple_of(g * 32, 32)
        at = [pl.ds(base + k, 8, ENTRIES) for k in range(ENTRIES)]
        targets, weights = regroup([target_in[a, :] for a in at], [weight[a, :] for a in at])
        for k in range(ENTRIES):
            target[at[k], :] = targets[k].astype(F32)
            weight[at[k], :] = weights[k]
        return carry

    lax.fori_loop(0, weight.shape[0] // 32, pair_up, 0, unroll=4)
    copies[2].wait()

    def send(t, carry):
        home = col[t]
        base = (home >> 1) * CHUNK + (home & 1) * 2
        at = pl.ds(pl.multiple_of(t * ENTRIES, ENTRIES), ENTRIES)
        out_ref[base] = weight[at, :].astype(BF16)
        out_ref[base + 1] = target[at, :].astype(BF16)
        return carry

    lax.fori_loop(0, tiles, send, 0, unroll=16)


def flux_kernel(
    owner_hbm, bits_hbm, atm_hbm, sent_hbm, out_hbm, slot_hbm,
    owner, slot, count, bits, atm, out, ocean, sems,
):
    blocks, fields, block = atm.shape
    words = bits.shape[0]
    copies = start_copies(((owner_hbm, owner), (bits_hbm, bits), (atm_hbm, atm)), sems)

    def clear(c, carry):
        count[c] = 0
        return carry

    lax.fori_loop(0, count.shape[0], clear, 0, unroll=16)
    copies[0].wait()

    def home(b, carry):
        to = owner[b]
        rank = count[to]
        count[to] = rank + 1
        slot[b] = 2 * to + rank
        return carry

    lax.fori_loop(0, blocks, home, 0, unroll=8)
    slots_out = pltpu.make_async_copy(slot, slot_hbm, sems.at[3])
    slots_out.start()

    copies[1].wait()
    column = lax.broadcasted_iota(I32, (blocks, block), 1)
    word = column // 30
    packed = jnp.concatenate([bits[...], jnp.zeros((8 - words, blocks), I32)], 0).T
    picked = jnp.zeros((blocks, block), I32)
    for w in range(words):
        picked = jnp.where(word == w, jnp.broadcast_to(packed[:, w : w + 1], (blocks, block)), picked)
    ocean[...] = jnp.right_shift(picked, column - word * 30) & 1

    copies[2].wait()
    field = lax.broadcasted_iota(I32, (8, block), 0)

    def fluxes_of(b):
        state = atm[b, 0:16, :].astype(F32)
        head = state[0:8]
        wind_east = head[0:1]
        wind_north = head[1:2]
        speed = jnp.sqrt(wind_east * wind_east + wind_north * wind_north + 0.25)
        drive = jnp.where(field < 2, head, pltpu.roll(head, 6, 0) - head)
        is_ocean = jnp.broadcast_to(ocean[pl.ds(b, 1), :], (8, block)) == 1
        head = jnp.where(is_ocean & (field < 4), (0.5 * speed) * drive, head)
        return jnp.concatenate([jnp.concatenate([head, state[8:16]], 0).astype(BF16), atm[b, 16:fields, :]], 0)

    def pair(p, carry):
        out[p] = jnp.concatenate([fluxes_of(2 * p), fluxes_of(2 * p + 1)], 0).T
        return carry

    lax.fori_loop(0, blocks // 2, pair, 0, unroll=4)
    fluxes_out = pltpu.make_async_copy(out, out_hbm, sems.at[4])
    fluxes_out.start()
    fluxes_out.wait()
    slots_out.wait()


def remap_kernel(
    ranks, slot_hbm, recv, flux_hbm, out_ref, owner_ref,
    slot, flux, sum_even, sum_odd, rows_vmem, rows, sems,
):
    pairs, block, _ = flux.shape
    fields = out_ref.shape[1]
    copies = start_copies(((slot_hbm, slot), (flux_hbm, flux)), sems)
    me = lax.axis_index("comp") * lax.axis_size("cpl") + lax.axis_index("cpl")
    entry_lane = lax.broadcasted_iota(I32, (ENTRIES, block), 1)

    def hear(c, carry):
        mine, device = carry
        info = recv[c * CHUNK + 4].astype(F32)
        moved = pltpu.roll(info, lax.rem(c - me + ranks, ranks), 1)
        return jnp.maximum(mine, jnp.where(entry_lane == c, moved, 0.0)), jnp.maximum(device, info)

    zeros = jnp.zeros((ENTRIES, block), F32)
    mine, device = lax.fori_loop(0, ranks, hear, (zeros, zeros), unroll=16)
    rows_vmem[...] = jnp.concatenate([mine, zeros], 0).astype(I32)
    rows_in = pltpu.make_async_copy(rows_vmem, rows, sems.at[2])
    rows_in.start()
    owner_ref[...] = jnp.concatenate([device, zeros], 0)
    sum_even[...] = jnp.zeros_like(sum_even)
    sum_odd[...] = jnp.zeros_like(sum_odd)
    column = lax.broadcasted_iota(I32, (block, block), 0).astype(F32).astype(BF16)
    nothing = jnp.zeros((), BF16)

    def spread(x):
        return jnp.broadcast_to(x, (block, block))

    def dense(b):
        home = slot[b]
        base = (home >> 1) * CHUNK + (home & 1) * 2
        weight = recv[base]
        target = recv[base + 1]

        def two(k):
            second = jnp.where(spread(target[k + 1 : k + 2]) == column, spread(weight[k + 1 : k + 2]), nothing)
            return jnp.where(spread(target[k : k + 1]) == column, spread(weight[k : k + 1]), second)

        return rows[home & 1, home >> 1], jnp.concatenate([two(0), two(2)], 1)

    def pair(p, carry):
        row0, dense0 = dense(2 * p)
        row1, dense1 = dense(2 * p + 1)
        both = flux[p]
        terms = jnp.dot(
            jnp.concatenate([dense0, dense1], 0), jnp.concatenate([both, both], 0), preferred_element_type=F32
        )
        sum_even[row0] += terms[:block]
        sum_odd[row1] += terms[block:]
        return carry

    for copy in copies:
        copy.wait()
    rows_in.wait()
    lax.fori_loop(0, pairs, pair, 0, unroll=pairs)
    for q in range(out_ref.shape[0]):
        total = sum_even[q] + pltpu.roll(sum_odd[q], fields, 1)
        out_ref[q] = total.T[:fields]


def permute_kernel(owner_ref, x_ref, out_ref):
    ranks, pieces, block = x_ref.shape
    rows = ranks * pieces
    source = lax.broadcasted_iota(I32, (block, rows), 0)
    spread = lax.broadcasted_iota(I32, (block, rows), 1) // pieces == source
    owner = jnp.dot(
        owner_ref[...].astype(BF16), spread.astype(F32).astype(BF16), preferred_element_type=F32
    )[2:3]
    half = lax.broadcasted_iota(I32, (1, rows), 1) % pieces
    wanted = (owner.astype(I32) - 1) * pieces + half
    chosen = lax.broadcasted_iota(I32, (rows, rows), 0) == jnp.broadcast_to(wanted, (rows, rows))
    chosen = chosen.astype(F32).astype(BF16)
    value = x_ref[...].reshape(rows, block)
    high = value.astype(BF16)
    left = value - high.astype(F32)
    middle = left.astype(BF16)
    low = (left - middle.astype(F32)).astype(BF16)
    total = jnp.dot(chosen, high, preferred_element_type=F32)
    total += jnp.dot(chosen, middle, preferred_element_type=F32)
    total += jnp.dot(chosen, low, preferred_element_type=F32)
    out_ref[...] = total.reshape(ranks, pieces, block)


def hbm():
    return pl.BlockSpec(memory_space=pltpu.HBM)


def vmem():
    return pl.BlockSpec(memory_space=pltpu.VMEM)


def in_hbm(x):
    return pltpu.with_memory_space_constraint(x, pltpu.HBM)


def exchange(x):
    return lax.all_to_all(x, AXES, split_axis=0, concat_axis=0, tiled=True)


def on_device(atm_fields, land_bits, coupler_owner, tile_col, tile_row, tile_weight, tile_target):
    ranks = lax.axis_size("comp") * lax.axis_size("cpl")
    blocks, fields, block = atm_fields.shape
    words = land_bits.shape[1]
    tiles = tile_col.shape[0]
    lines = tiles * ENTRIES
    ocean_blocks = blocks // RATIO
    params = pltpu.CompilerParams(vmem_limit_bytes=VMEM_LIMIT)

    send = pl.pallas_call(
        lambda *refs: pack_kernel(ranks, ocean_blocks, *refs),
        out_shape=jax.ShapeDtypeStruct((ranks * CHUNK, ENTRIES, block), BF16),
        in_specs=[hbm()] * 5,
        out_specs=vmem(),
        scratch_shapes=[
            pltpu.SMEM((tiles,), I32),
            pltpu.VMEM((tiles // block, block), I32),
            pltpu.VMEM((tiles // block, block), I32),
            pltpu.VMEM((lines, block), BF16),
            pltpu.VMEM((lines, block), I32),
            pltpu.VMEM((lines, block), F32),
            pltpu.VMEM((lines, block), F32),
            pltpu.SemaphoreType.DMA((5,)),
        ],
        compiler_params=params,
        name="pack",
    )(
        in_hbm(tile_col),
        in_hbm(tile_col.reshape(tiles // block, block)),
        in_hbm(tile_row.reshape(tiles // block, block)),
        in_hbm(tile_weight.reshape(lines, block)),
        in_hbm(tile_target.reshape(lines, block)),
    )
    recv = exchange(send)

    fluxes, slot = pl.pallas_call(
        flux_kernel,
        out_shape=(pltpu.HBM((blocks // 2, block, 2 * fields), BF16), pltpu.HBM((blocks,), I32)),
        in_specs=[hbm()] * 3 + [pl.BlockSpec(memory_space=pl.ANY)],
        out_specs=(hbm(), hbm()),
        scratch_shapes=[
            pltpu.SMEM((blocks,), I32),
            pltpu.SMEM((blocks,), I32),
            pltpu.SMEM((ranks,), I32),
            pltpu.VMEM((words, blocks), I32),
            pltpu.VMEM((blocks, fields, block), BF16),
            pltpu.VMEM((blocks // 2, block, 2 * fields), BF16),
            pltpu.VMEM((blocks, block), I32),
            pltpu.SemaphoreType.DMA((5,)),
        ],
        compiler_params=params,
        cost_estimate=pl.CostEstimate(flops=10_000_000, bytes_accessed=4_000_000, transcendentals=0),
        name="flux",
    )(in_hbm(coupler_owner), in_hbm(land_bits.T), in_hbm(atm_fields), send)

    sums, owner = pl.pallas_call(
        lambda *refs: remap_kernel(ranks, *refs),
        out_shape=(
            jax.ShapeDtypeStruct((ocean_blocks, fields, block), F32),
            jax.ShapeDtypeStruct((8, block), F32),
        ),
        in_specs=[hbm(), vmem(), hbm()],
        out_specs=(vmem(), vmem()),
        scratch_shapes=[
            pltpu.SMEM((blocks,), I32),
            pltpu.VMEM((blocks // 2, block, 2 * fields), BF16),
            pltpu.VMEM((ocean_blocks, block, 2 * fields), F32),
            pltpu.VMEM((ocean_blocks, block, 2 * fields), F32),
            pltpu.VMEM((8, block), I32),
            pltpu.SMEM((8, block), I32),
            pltpu.SemaphoreType.DMA((3,)),
        ],
        compiler_params=params,
        name="remap",
    )(in_hbm(slot), recv, in_hbm(fluxes))

    pieces = ocean_blocks * fields // ranks
    spread = exchange(sums.reshape(ranks, pieces, block))
    turned = pl.pallas_call(
        permute_kernel,
        out_shape=jax.ShapeDtypeStruct(spread.shape, F32),
        in_specs=[vmem(), vmem()],
        out_specs=vmem(),
        compiler_params=params,
        name="permute",
    )(owner, spread)
    return exchange(turned).reshape(ocean_blocks, fields, block)


def solution(mesh):
    in_specs = (
        P(AXES, None, None),
        P(AXES, None),
        P(AXES),
        P(AXES),
        P(AXES),
        P(AXES, None, None),
        P(AXES, None, None),
    )
    return jax.shard_map(
        on_device, mesh=mesh, in_specs=in_specs, out_specs=P(AXES, None, None), check_vma=False
    )
```

time: 76.7 us -> 63.6 us (0.83)
  local copies, waits for them, and re-layouts: 7.19 us -> 0.66 us
  Pallas kernels: 18.5 us -> 12.3 us
    unnamed x20 -> x1, local copies, waits for them, and re-layouts: 7.19 us -> 0.66 us
    pallas_call x2, Pallas kernels: 13.8 us -> 8.89 us  [the longest x1 4.71 us: on_device(): pl.pallas_call(flux_kernel, out_shape=(pltpu.HBM((blocks // 2, block, 2 *...]
    pallas_call x1, Pallas kernels: 4.29 us -> 2.98 us  [on_device(): pl.pallas_call(lambda *refs: pack_kernel(ranks, ocean_blocks, *refs), out...]
  transfers between devices with their start and end apart: 1 -> 1, of which waited for: 1 -> 1; matrix products, arithmetic and copies ran while one was open for 0% -> 0% of each run, Pallas kernels for 4% -> 7%
where the time goes in v2:
time: 63.6 us; the launch traced here: 63.3 us
  blocking collectives  28.3 us (44%)
  Pallas kernels  12.3 us (19%)
  starting transfers between devices  11.5 us (18%)
  waiting for transfers between devices  10.5 us (17%)
  local copies, waits for them, and re-layouts  0.66 us (1%)
    all_to_all x2, blocking collectives, exchange(): return lax.all_to_all(x, AXES, split_axis=0, concat_axis=0, tiled=True)  28.3 us
    all_to_all x1, starting transfers between devices, exchange(): return lax.all_to_all(x, AXES, split_axis=0, concat_axis=0, tiled=True)  11.5 us
    all_to_all x1, waiting for transfers between devices, exchange(): return lax.all_to_all(x, AXES, split_axis=0, concat_axis=0, tiled=True)  10.5 us
    pallas_call x1, Pallas kernels, on_device(): pl.pallas_call(flux_kernel, out_shape=(pltpu.HBM((blocks // 2, block, 2 *...  4.71 us
    pallas_call x1, Pallas kernels, on_device(): pl.pallas_call(lambda *refs: remap_kernel(ranks, *refs), out_shape=(jax.S...  4.18 us
    pallas_call x1, Pallas kernels, on_device(): pl.pallas_call(lambda *refs: pack_kernel(ranks, ocean_blocks, *refs), out...  2.98 us
  transfers between devices with their start and end apart: 1, of which 1 were waited for; matrix products, arithmetic and copies ran while one was open for 0% of the time, Pallas kernels for 7%

profile of v2, /device:TPU:1, one launch (start us, length us, event | category | flops | bytes accessed | tf_op | source)
XLA Modules:
  0.0 63.3 jit_solution(12108728108904861631)
XLA Ops:
  0.0 3.0 %pack.1.sent_hbm = bf16[640,4,128]{2,1,0:T(4,128)(2,1)} custom-call(s32[256]{0:T(256)} %refs_0_.1, s32[2,128]{1,0:T(2,128)} %bitcast.12, s32[2,128]{1,0:T(2,128)} %bitcast.13, bf16[1024,128]{1,0:T(8,128)(2,1)} %bitcast.10, s32[1024,128]{1,0:T(8,128)} %bitcast.8), custom_call_target="tpu_custom_call" | custom-call | tf_op jit(solution)/shard_map/pack/pallas_call | solution.py:295
  3.0 11.5 %all-to-all-start = ((bf16[640,4,128]{2,1,0:T(4,128)(2,1)}), bf16[640,4,128]{2,1,0:T(4,128)(2,1)S(1)}, u32[]{:S(2)}, u32[]{:S(2)}) async-start(bf16[640,4,128]{2,1,0:T(4,128)(2,1)} %pack.1.sent_hbm), calls=%async_computation | async-start | bytes 1310720 | tf_op jit(solution)/shard_map/all_to_all | solution.py:283
  14.5 4.7 %flux.1 = (bf16[64,128,128]{2,1,0:T(8,128)(2,1)}, s32[128]{0:T(128)}) custom-call(s32[128]{0:T(128)} %owner_hbm.1, s32[5,128]{1,0:T(8,128)} %bitcast.11, bf16[128,64,128]{2,1,0:T(8,128)(2,1)} %atm_hbm.1, bf16[640,4,128]{2,1,0:T(4,128)(2,1)} %pack.1.sent_hbm), custom_call_target="tpu_custom_call" | custom-call | flops 10000000 | bytes 4000000 | tf_op jit(solution)/shard_map/flux/pallas_call | solution.py:321
  19.2 10.5 %all-to-all-done.refs_1_ = bf16[640,4,128]{2,1,0:T(4,128)(2,1)S(1)} async-done(((bf16[640,4,128]{2,1,0:T(4,128)(2,1)}), bf16[640,4,128]{2,1,0:T(4,128)(2,1)S(1)}, u32[]{:S(2)}, u32[]{:S(2)}) %all-to-all-start) | async-done | bytes 655392 | tf_op jit(solution)/shard_map/all_to_all | solution.py:283
  29.7 4.2 %remap.1 = (f32[4,64,128]{2,1,0:T(8,128)S(1)}, f32[8,128]{1,0:T(8,128)S(1)}) custom-call(s32[128]{0:T(128)} %get-tuple-element.9.refs_0_, bf16[640,4,128]{2,1,0:T(4,128)(2,1)S(1)} %all-to-all-done.refs_1_, bf16[64,128,128]{2,1,0:T(8,128)(2,1)} %get-tuple-element.10.refs_2_), custom_call_target="tpu_custom_call" | custom-call | tf_op jit(solution)/shard_map/remap/pallas_call | solution.py:341
  33.9 14.1 %all_to_all.15.x_ref = f32[128,2,128]{2,1,0:T(2,128)S(1)} all-to-all(f32[128,2,128]{2,1,0:T(2,128)S(1)} %bitcast.7), channel_id=1, replica_groups=mesh['comp'=8,'cpl'=16] {'comp','cpl'}, dimensions={0} | all-to-all | bytes 262144 | tf_op jit(solution)/shard_map/all_to_all | solution.py:283
  48.0 0.4 permute.1
  48.4 14.2 %all_to_all.16 = f32[128,2,128]{2,1,0:T(2,128)S(1)} all-to-all(f32[128,2,128]{2,1,0:T(2,128)S(1)} %permute.1), channel_id=1, replica_groups=mesh['comp'=8,'cpl'=16] {'comp','cpl'}, dimensions={0} | all-to-all | bytes 262144 | tf_op jit(solution)/shard_map/all_to_all | solution.py:283
  62.6 0.7 %copy.9 = f32[4,64,128]{2,1,0:T(8,128)} copy(f32[4,64,128]{2,1,0:T(8,128)S(1)} %bitcast.9) | data formatting | bytes 262144
Async XLA Ops:
  3.0 26.7 %all-to-all-start = ((bf16[640,4,128]{2,1,0:T(4,128)(2,1)}), bf16[640,4,128]{2,1,0:T(4,128)(2,1)S(1)}, u32[]{:S(2)}, u32[]{:S(2)}) async-start(bf16[640,4,128]{2,1,0:T(4,128)(2,1)} %pack.1.sent_hbm), calls=%async_computation | async-start | bytes 1310720 | tf_op jit(solution)/shard_map/all_to_all | solution.py:283

commit v3 on v2

--- a/solution.py
+++ b/solution.py
@@ -8,7 +8,9 @@
 AXES = ("comp", "cpl")
 ENTRIES = 4
 RATIO = 32
-CHUNK = 5
+CHUNK = 9
+TILE_PAIRS = 4
+STAGES = 4
 VMEM_LIMIT = 24 * 1024 * 1024
 BF16 = jnp.bfloat16
 F32 = jnp.float32
@@ -55,14 +57,23 @@
     out_ref, col, col2, row2, weight_in, target_in, weight, target, sems,
 ):
     tiles = col.shape[0]
-    block = weight.shape[1]
+    lines, block = weight.shape
     halves = tiles // block
-    copies = start_copies(
-        ((col2_hbm, col2), (row2_hbm, row2), (col_hbm, col), (weight_hbm, weight_in), (target_hbm, target_in)), sems
-    )
-
-    copies[0].wait()
-    copies[1].wait()
+    stage_lines = lines // STAGES
+    stage_tiles = tiles // STAGES
+    col2_copy, row2_copy, col_copy = start_copies(((col2_hbm, col2), (row2_hbm, row2), (col_hbm, col)), sems)
+    stages = []
+    for i in range(STAGES):
+        part = pl.ds(i * stage_lines, stage_lines)
+        stages.append(
+            start_copies(
+                ((weight_hbm.at[part], weight_in.at[part]), (target_hbm.at[part], target_in.at[part])),
+                sems.at[pl.ds(3 + 2 * i, 2)],
+            )
+        )
+
+    col2_copy.wait()
+    row2_copy.wait()
     slot = (col2[...] & 1) * ranks + (col2[...] >> 1)
     entry = lax.broadcasted_iota(I32, (8, block), 0)
     place = lax.broadcasted_iota(I32, (tiles, block), 0)
@@ -77,27 +88,26 @@
     found = lax.dot_general(
         jnp.concatenate(values, 1), jnp.concatenate(onehot, 1), ROWS_WITH_ROWS, preferred_element_type=F32
     )
-    entry = entry[:ENTRIES]
-    local0 = jnp.broadcast_to(found[0:1, :ranks], (ENTRIES, block))
-    local1 = jnp.broadcast_to(found[0:1, ranks:], (ENTRIES, block))
-    device = jnp.broadcast_to(jnp.maximum(found[1:2, :ranks], found[1:2, ranks:]), (ENTRIES, block))
-    info = jnp.where(entry == 0, local0, jnp.where(entry == 1, local1, device)).astype(BF16)
-
-    def tell(s, carry):
-        out_ref[s * CHUNK + 4] = info
-        return carry
-
-    lax.fori_loop(0, ranks, tell, 0, unroll=16)
-
-    copies[3].wait()
+    device = jnp.maximum(found[1:2, :ranks], found[1:2, ranks:])
+    low_lanes = lax.broadcasted_iota(I32, (1, block), 1) < ranks // 2
+    first, second = found[0:1, :ranks], found[0:1, ranks:]
+    locals_of = (
+        jnp.where(low_lanes, first, pltpu.roll(second, ranks // 2, 1)),
+        jnp.where(low_lanes, pltpu.roll(first, ranks // 2, 1), second),
+    )
+    for h in range(2):
+        info = jnp.concatenate([device, locals_of[h]], 0).astype(BF16)
+
+        def tell(s, carry, info=info):
+            out_ref[s * CHUNK + 2 * TILE_PAIRS] = info
+            return carry
+
+        lax.fori_loop(h * ranks // 2, (h + 1) * ranks // 2, tell, 0, unroll=16)
 
     def widen(g, carry):
         at = pl.ds(pl.multiple_of(g * 16, 16), 16)
         weight[at] = weight_in[at].astype(F32)
         return carry
-
-    lax.fori_loop(0, weight.shape[0] // 16, widen, 0, unroll=8)
-    copies[4].wait()
 
     def pair_up(g, carry):
         base = pl.multiple_of(g * 32, 32)
@@ -108,23 +118,33 @@
             weight[at[k], :] = weights[k]
         return carry
 
-    lax.fori_loop(0, weight.shape[0] // 32, pair_up, 0, unroll=4)
-    copies[2].wait()
-
     def send(t, carry):
         home = col[t]
-        base = (home >> 1) * CHUNK + (home & 1) * 2
-        at = pl.ds(pl.multiple_of(t * ENTRIES, ENTRIES), ENTRIES)
-        out_ref[base] = weight[at, :].astype(BF16)
-        out_ref[base + 1] = target[at, :].astype(BF16)
-        return carry
-
-    lax.fori_loop(0, tiles, send, 0, unroll=16)
+        base = (home >> 1) * CHUNK + (home & 1) * TILE_PAIRS
+        line = pl.multiple_of(t * ENTRIES, ENTRIES)
+        for h in range(2):
+            at = pl.ds(line + 2 * h, 2)
+            out_ref[base + h] = weight[at, :].astype(BF16)
+            out_ref[base + 2 + h] = target[at, :].astype(BF16)
+        return carry
+
+    def each(part, size, body, unroll):
+        count = stage_lines // size
+        lax.fori_loop(part * count, (part + 1) * count, body, 0, unroll=unroll)
+
+    for i in range(STAGES):
+        stages[i][0].wait()
+        each(i, 16, widen, 16)
+        stages[i][1].wait()
+        each(i, 32, pair_up, 8)
+        if i == 0:
+            col_copy.wait()
+        each(i, ENTRIES, send, stage_tiles)
 
 
 def flux_kernel(
-    owner_hbm, bits_hbm, atm_hbm, sent_hbm, out_hbm, slot_hbm,
-    owner, slot, count, bits, atm, out, ocean, sems,
+    owner_hbm, bits_hbm, atm_hbm, sent_hbm, out, slot_hbm,
+    owner, slot, count, bits, atm, ocean, sems,
 ):
     blocks, fields, block = atm.shape
     words = bits.shape[0]
@@ -176,34 +196,36 @@
         return carry
 
     lax.fori_loop(0, blocks // 2, pair, 0, unroll=4)
-    fluxes_out = pltpu.make_async_copy(out, out_hbm, sems.at[4])
-    fluxes_out.start()
-    fluxes_out.wait()
     slots_out.wait()
 
 
 def remap_kernel(
-    ranks, slot_hbm, recv, flux_hbm, out_ref, owner_ref,
-    slot, flux, sum_even, sum_odd, rows_vmem, rows, sems,
+    ranks, slot_hbm, recv, flux, out_ref, owner_ref,
+    slot, sum_even, sum_odd, rows_vmem, rows, sems,
 ):
     pairs, block, _ = flux.shape
     fields = out_ref.shape[1]
-    copies = start_copies(((slot_hbm, slot), (flux_hbm, flux)), sems)
+    copies = start_copies(((slot_hbm, slot),), sems)
     me = lax.axis_index("comp") * lax.axis_size("cpl") + lax.axis_index("cpl")
-    entry_lane = lax.broadcasted_iota(I32, (ENTRIES, block), 1)
+    lane = lax.broadcasted_iota(I32, (2, block), 1)
+    other = ranks // 2
+    mine = lax.rem(me, other)
 
     def hear(c, carry):
-        mine, device = carry
-        info = recv[c * CHUNK + 4].astype(F32)
-        moved = pltpu.roll(info, lax.rem(c - me + ranks, ranks), 1)
-        return jnp.maximum(mine, jnp.where(entry_lane == c, moved, 0.0)), jnp.maximum(device, info)
-
-    zeros = jnp.zeros((ENTRIES, block), F32)
-    mine, device = lax.fori_loop(0, ranks, hear, (zeros, zeros), unroll=16)
-    rows_vmem[...] = jnp.concatenate([mine, zeros], 0).astype(I32)
-    rows_in = pltpu.make_async_copy(rows_vmem, rows, sems.at[2])
+        local0, local1, device = carry
+        info = recv[c * CHUNK + 2 * TILE_PAIRS].astype(F32)
+        moved = pltpu.roll(info, lax.rem(c - mine + ranks, ranks), 1)
+        local0 = jnp.maximum(local0, jnp.where(lane == c, moved, 0.0))
+        local1 = jnp.maximum(local1, jnp.where(lane == (c ^ other), moved, 0.0))
+        return local0, local1, jnp.maximum(device, info)
+
+    zeros = jnp.zeros((2, block), F32)
+    local0, local1, device = lax.fori_loop(0, ranks, hear, (zeros, zeros, zeros), unroll=ranks)
+    padding = jnp.zeros((6, block), F32)
+    rows_vmem[...] = jnp.concatenate([local0[1:2], local1[1:2], padding], 0).astype(I32)
+    rows_in = pltpu.make_async_copy(rows_vmem, rows, sems.at[1])
     rows_in.start()
-    owner_ref[...] = jnp.concatenate([device, zeros], 0)
+    owner_ref[...] = jnp.concatenate([device, padding], 0)
     sum_even[...] = jnp.zeros_like(sum_even)
     sum_odd[...] = jnp.zeros_like(sum_odd)
     column = lax.broadcasted_iota(I32, (block, block), 0).astype(F32).astype(BF16)
@@ -214,15 +236,17 @@
 
     def dense(b):
         home = slot[b]
-        base = (home >> 1) * CHUNK + (home & 1) * 2
-        weight = recv[base]
-        target = recv[base + 1]
-
-        def two(k):
-            second = jnp.where(spread(target[k + 1 : k + 2]) == column, spread(weight[k + 1 : k + 2]), nothing)
-            return jnp.where(spread(target[k : k + 1]) == column, spread(weight[k : k + 1]), second)
-
-        return rows[home & 1, home >> 1], jnp.concatenate([two(0), two(2)], 1)
+        source = home >> 1
+        rank = home & 1
+        base = source * CHUNK + rank * TILE_PAIRS
+
+        def two(h):
+            weight = recv[base + h]
+            target = recv[base + 2 + h]
+            second = jnp.where(spread(target[1:2]) == column, spread(weight[1:2]), nothing)
+            return jnp.where(spread(target[0:1]) == column, spread(weight[0:1]), second)
+
+        return rows[rank, source ^ (rank * other)], jnp.concatenate([two(0), two(1)], 1)
 
     def pair(p, carry):
         row0, dense0 = dense(2 * p)
@@ -251,7 +275,7 @@
     spread = lax.broadcasted_iota(I32, (block, rows), 1) // pieces == source
     owner = jnp.dot(
         owner_ref[...].astype(BF16), spread.astype(F32).astype(BF16), preferred_element_type=F32
-    )[2:3]
+    )[0:1]
     half = lax.broadcasted_iota(I32, (1, rows), 1) % pieces
     wanted = (owner.astype(I32) - 1) * pieces + half
     chosen = lax.broadcasted_iota(I32, (rows, rows), 0) == jnp.broadcast_to(wanted, (rows, rows))
@@ -294,7 +318,7 @@
 
     send = pl.pallas_call(
         lambda *refs: pack_kernel(ranks, ocean_blocks, *refs),
-        out_shape=jax.ShapeDtypeStruct((ranks * CHUNK, ENTRIES, block), BF16),
+        out_shape=jax.ShapeDtypeStruct((ranks * CHUNK, 2, block), BF16),
         in_specs=[hbm()] * 5,
         out_specs=vmem(),
         scratch_shapes=[
@@ -305,7 +329,7 @@
             pltpu.VMEM((lines, block), I32),
             pltpu.VMEM((lines, block), F32),
             pltpu.VMEM((lines, block), F32),
-            pltpu.SemaphoreType.DMA((5,)),
+            pltpu.SemaphoreType.DMA((3 + 2 * STAGES,)),
         ],
         compiler_params=params,
         name="pack",
@@ -320,18 +344,17 @@
 
     fluxes, slot = pl.pallas_call(
         flux_kernel,
-        out_shape=(pltpu.HBM((blocks // 2, block, 2 * fields), BF16), pltpu.HBM((blocks,), I32)),
+        out_shape=(pltpu.VMEM((blocks // 2, block, 2 * fields), BF16), pltpu.HBM((blocks,), I32)),
         in_specs=[hbm()] * 3 + [pl.BlockSpec(memory_space=pl.ANY)],
-        out_specs=(hbm(), hbm()),
+        out_specs=(vmem(), hbm()),
         scratch_shapes=[
             pltpu.SMEM((blocks,), I32),
             pltpu.SMEM((blocks,), I32),
             pltpu.SMEM((ranks,), I32),
             pltpu.VMEM((words, blocks), I32),
             pltpu.VMEM((blocks, fields, block), BF16),
-            pltpu.VMEM((blocks // 2, block, 2 * fields), BF16),
             pltpu.VMEM((blocks, block), I32),
-            pltpu.SemaphoreType.DMA((5,)),
+            pltpu.SemaphoreType.DMA((4,)),
         ],
         compiler_params=params,
         cost_estimate=pl.CostEstimate(flops=10_000_000, bytes_accessed=4_000_000, transcendentals=0),
@@ -344,20 +367,19 @@
             jax.ShapeDtypeStruct((ocean_blocks, fields, block), F32),
             jax.ShapeDtypeStruct((8, block), F32),
         ),
-        in_specs=[hbm(), vmem(), hbm()],
+        in_specs=[hbm(), vmem(), vmem()],
         out_specs=(vmem(), vmem()),
         scratch_shapes=[
             pltpu.SMEM((blocks,), I32),
-            pltpu.VMEM((blocks // 2, block, 2 * fields), BF16),
             pltpu.VMEM((ocean_blocks, block, 2 * fields), F32),
             pltpu.VMEM((ocean_blocks, block, 2 * fields), F32),
             pltpu.VMEM((8, block), I32),
             pltpu.SMEM((8, block), I32),
-            pltpu.SemaphoreType.DMA((3,)),
+            pltpu.SemaphoreType.DMA((2,)),
         ],
         compiler_params=params,
         name="remap",
-    )(in_hbm(slot), recv, in_hbm(fluxes))
+    )(in_hbm(slot), recv, fluxes)
 
     pieces = ocean_blocks * fields // ranks
     spread = exchange(sums.reshape(ranks, pieces, block))

time: 63.6 us -> 61.8 us (0.972)
  Pallas kernels: 12.3 us -> 9.87 us
  waiting for transfers between devices: 10.5 us -> 11.2 us
    pallas_call x1, Pallas kernels: 4.71 us -> 3.37 us  [on_device(): pl.pallas_call(flux_kernel, out_shape=(pltpu.VMEM((blocks // 2, block, 2...]
    pallas_call x1, Pallas kernels: 4.18 us -> 3.48 us  [on_device(): pl.pallas_call(lambda *refs: remap_kernel(ranks, *refs), out_shape=(jax.S...]
    all_to_all x1, waiting for transfers between devices: 10.5 us -> 11.2 us  [exchange(): return lax.all_to_all(x, AXES, split_axis=0, concat_axis=0, tiled=True)]
  transfers between devices with their start and end apart: 1 -> 1, of which waited for: 1 -> 1; matrix products, arithmetic and copies ran while one was open for 0% -> 0% of each run, Pallas kernels for 7% -> 5%
where the time goes in v3:
time: 61.8 us; the launch traced here: 61.6 us
  blocking collectives  28.4 us (46%)
  starting transfers between devices  11.5 us (19%)
  waiting for transfers between devices  11.2 us (18%)
  Pallas kernels  9.87 us (16%)
  local copies, waits for them, and re-layouts  0.66 us (1%)
    all_to_all x2, blocking collectives, exchange(): return lax.all_to_all(x, AXES, split_axis=0, concat_axis=0, tiled=True)  28.4 us
    all_to_all x1, starting transfers between devices, exchange(): return lax.all_to_all(x, AXES, split_axis=0, concat_axis=0, tiled=True)  11.5 us
    all_to_all x1, waiting for transfers between devices, exchange(): return lax.all_to_all(x, AXES, split_axis=0, concat_axis=0, tiled=True)  11.2 us
    pallas_call x1, Pallas kernels, on_device(): pl.pallas_call(lambda *refs: remap_kernel(ranks, *refs), out_shape=(jax.S...  3.48 us
    pallas_call x1, Pallas kernels, on_device(): pl.pallas_call(flux_kernel, out_shape=(pltpu.VMEM((blocks // 2, block, 2...  3.37 us
    pallas_call x1, Pallas kernels, on_device(): pl.pallas_call(lambda *refs: pack_kernel(ranks, ocean_blocks, *refs), out...  2.62 us
  transfers between devices with their start and end apart: 1, of which 1 were waited for; matrix products, arithmetic and copies ran while one was open for 0% of the time, Pallas kernels for 5%

profile of v3, /device:TPU:1, one launch (start us, length us, event | category | flops | bytes accessed | tf_op | source)
XLA Modules:
  0.0 61.6 jit_solution(16062166845282598862)
XLA Ops:
  0.0 2.6 %pack.1.sent_hbm = bf16[1152,2,128]{2,1,0:T(2,128)(2,1)} custom-call(s32[256]{0:T(256)} %refs_0_.1, s32[2,128]{1,0:T(2,128)} %bitcast.12, s32[2,128]{1,0:T(2,128)} %bitcast.13, bf16[1024,128]{1,0:T(8,128)(2,1)} %bitcast.10, s32[1024,128]{1,0:T(8,128)} %bitcast.8), custom_call_target="tpu_custom_call" | custom-call | tf_op jit(solution)/shard_map/pack/pallas_call | solution.py:319
  2.6 11.5 %all-to-all-start = ((bf16[1152,2,128]{2,1,0:T(2,128)(2,1)}), bf16[1152,2,128]{2,1,0:T(2,128)(2,1)S(1)}, u32[]{:S(2)}, u32[]{:S(2)}) async-start(bf16[1152,2,128]{2,1,0:T(2,128)(2,1)} %pack.1.sent_hbm), calls=%async_computation | async-start | bytes 1179648 | tf_op jit(solution)/shard_map/all_to_all | solution.py:307
  14.1 3.4 %flux.1 = (bf16[64,128,128]{2,1,0:T(8,128)(2,1)S(1)}, s32[128]{0:T(128)}) custom-call(s32[128]{0:T(128)} %owner_hbm.1, s32[5,128]{1,0:T(8,128)} %bitcast.11, bf16[128,64,128]{2,1,0:T(8,128)(2,1)} %atm_hbm.1, bf16[1152,2,128]{2,1,0:T(2,128)(2,1)} %pack.1.sent_hbm), custom_call_target="tpu_custom_call" | custom-call | flops 10000000 | bytes 4000000 | tf_op jit(solution)/shard_map/flux/pallas_call | solution.py:345
  17.5 11.2 %all-to-all-done.refs_1_ = bf16[1152,2,128]{2,1,0:T(2,128)(2,1)S(1)} async-done(((bf16[1152,2,128]{2,1,0:T(2,128)(2,1)}), bf16[1152,2,128]{2,1,0:T(2,128)(2,1)S(1)}, u32[]{:S(2)}, u32[]{:S(2)}) %all-to-all-start) | async-done | bytes 589856 | tf_op jit(solution)/shard_map/all_to_all | solution.py:307
  28.7 3.5 %remap.1 = (f32[4,64,128]{2,1,0:T(8,128)S(1)}, f32[8,128]{1,0:T(8,128)S(1)}) custom-call(s32[128]{0:T(128)} %get-tuple-element.9.refs_0_, bf16[1152,2,128]{2,1,0:T(2,128)(2,1)S(1)} %all-to-all-done.refs_1_, bf16[64,128,128]{2,1,0:T(8,128)(2,1)S(1)} %get-tuple-element.10.refs_2_), custom_call_target="tpu_custom_call" | custom-call | tf_op jit(solution)/shard_map/remap/pallas_call | solution.py:364
  32.2 14.2 %all_to_all.15.x_ref = f32[128,2,128]{2,1,0:T(2,128)S(1)} all-to-all(f32[128,2,128]{2,1,0:T(2,128)S(1)} %bitcast.7), channel_id=1, replica_groups=mesh['comp'=8,'cpl'=16] {'comp','cpl'}, dimensions={0} | all-to-all | bytes 262144 | tf_op jit(solution)/shard_map/all_to_all | solution.py:307
  46.3 0.4 permute.1
  46.7 14.2 %all_to_all.16 = f32[128,2,128]{2,1,0:T(2,128)S(1)} all-to-all(f32[128,2,128]{2,1,0:T(2,128)S(1)} %permute.1), channel_id=1, replica_groups=mesh['comp'=8,'cpl'=16] {'comp','cpl'}, dimensions={0} | all-to-all | bytes 262144 | tf_op jit(solution)/shard_map/all_to_all | solution.py:307
  60.9 0.7 %copy.9 = f32[4,64,128]{2,1,0:T(8,128)} copy(f32[4,64,128]{2,1,0:T(8,128)S(1)} %bitcast.9) | data formatting | bytes 262144
Async XLA Ops:
  2.6 26.0 %all-to-all-start = ((bf16[1152,2,128]{2,1,0:T(2,128)(2,1)}), bf16[1152,2,128]{2,1,0:T(2,128)(2,1)S(1)}, u32[]{:S(2)}, u32[]{:S(2)}) async-start(bf16[1152,2,128]{2,1,0:T(2,128)(2,1)} %pack.1.sent_hbm), calls=%async_computation | async-start | bytes 1179648 | tf_op jit(solution)/shard_map/all_to_all | solution.py:307

commit v4 on v3

--- a/solution.py
+++ b/solution.py
@@ -143,30 +143,23 @@
 
 
 def flux_kernel(
-    owner_hbm, bits_hbm, atm_hbm, sent_hbm, out, slot_hbm,
-    owner, slot, count, bits, atm, ocean, sems,
+    owner_hbm, bits_hbm, atm_hbm, sent_hbm, out, place_ref, onehot_ref,
+    owner, bits, atm, ocean, sems,
 ):
     blocks, fields, block = atm.shape
+    slots = onehot_ref.shape[0]
+    ranks = slots // 2
     words = bits.shape[0]
     copies = start_copies(((owner_hbm, owner), (bits_hbm, bits), (atm_hbm, atm)), sems)
 
-    def clear(c, carry):
-        count[c] = 0
-        return carry
-
-    lax.fori_loop(0, count.shape[0], clear, 0, unroll=16)
     copies[0].wait()
-
-    def home(b, carry):
-        to = owner[b]
-        rank = count[to]
-        count[to] = rank + 1
-        slot[b] = 2 * to + rank
-        return carry
-
-    lax.fori_loop(0, blocks, home, 0, unroll=8)
-    slots_out = pltpu.make_async_copy(slot, slot_hbm, sems.at[3])
-    slots_out.start()
+    to = jnp.broadcast_to(owner[...], (blocks, blocks))
+    earlier = lax.broadcasted_iota(I32, (blocks, blocks), 0) < lax.broadcasted_iota(I32, (blocks, blocks), 1)
+    rank = jnp.sum(jnp.where((to == to.T) & earlier, 1, 0), axis=0, keepdims=True)
+    place_ref[...] = jnp.broadcast_to(owner[...] * CHUNK + rank * TILE_PAIRS, place_ref.shape)
+    slot = jnp.broadcast_to(rank * ranks + owner[...], (slots, blocks))
+    same = lax.broadcasted_iota(I32, (slots, blocks), 0) == slot
+    onehot_ref[...] = jnp.where(same, 1.0, 0.0).astype(BF16)
 
     copies[1].wait()
     column = lax.broadcasted_iota(I32, (blocks, block), 1)
@@ -196,16 +189,13 @@
         return carry
 
     lax.fori_loop(0, blocks // 2, pair, 0, unroll=4)
-    slots_out.wait()
 
 
 def remap_kernel(
-    ranks, slot_hbm, recv, flux, out_ref, owner_ref,
-    slot, sum_even, sum_odd, rows_vmem, rows, sems,
+    ranks, place_ref, onehot_ref, recv, flux, out_ref, owner_ref, sum_even, sum_odd,
 ):
     pairs, block, _ = flux.shape
     fields = out_ref.shape[1]
-    copies = start_copies(((slot_hbm, slot),), sems)
     me = lax.axis_index("comp") * lax.axis_size("cpl") + lax.axis_index("cpl")
     lane = lax.broadcasted_iota(I32, (2, block), 1)
     other = ranks // 2
@@ -221,11 +211,12 @@
 
     zeros = jnp.zeros((2, block), F32)
     local0, local1, device = lax.fori_loop(0, ranks, hear, (zeros, zeros, zeros), unroll=ranks)
-    padding = jnp.zeros((6, block), F32)
-    rows_vmem[...] = jnp.concatenate([local0[1:2], local1[1:2], padding], 0).astype(I32)
-    rows_in = pltpu.make_async_copy(rows_vmem, rows, sems.at[1])
-    rows_in.start()
-    owner_ref[...] = jnp.concatenate([device, padding], 0)
+    owner_ref[...] = jnp.concatenate([device, jnp.zeros((6, block), F32)], 0)
+    by_slot = jnp.concatenate([local0[1:2], pltpu.roll(local1, other, 1)[1:2]], 1)
+    by_slot = jnp.broadcast_to(by_slot, (8, 2 * ranks)).astype(BF16)
+    rows = jnp.dot(by_slot, onehot_ref[...], preferred_element_type=F32).astype(I32)
+    shift = out_ref.shape[0].bit_length() - 1
+    both_of = place_ref[...] * out_ref.shape[0] + rows
     sum_even[...] = jnp.zeros_like(sum_even)
     sum_odd[...] = jnp.zeros_like(sum_odd)
     column = lax.broadcasted_iota(I32, (block, block), 0).astype(F32).astype(BF16)
@@ -234,35 +225,26 @@
     def spread(x):
         return jnp.broadcast_to(x, (block, block))
 
-    def dense(b):
-        home = slot[b]
-        source = home >> 1
-        rank = home & 1
-        base = source * CHUNK + rank * TILE_PAIRS
-
+    def dense(base):
         def two(h):
             weight = recv[base + h]
             target = recv[base + 2 + h]
             second = jnp.where(spread(target[1:2]) == column, spread(weight[1:2]), nothing)
             return jnp.where(spread(target[0:1]) == column, spread(weight[0:1]), second)
 
-        return rows[rank, source ^ (rank * other)], jnp.concatenate([two(0), two(1)], 1)
-
-    def pair(p, carry):
-        row0, dense0 = dense(2 * p)
-        row1, dense1 = dense(2 * p + 1)
+        return jnp.concatenate([two(0), two(1)], 1)
+
+    for p in range(pairs):
+        at0 = both_of[0, 2 * p]
+        at1 = both_of[0, 2 * p + 1]
         both = flux[p]
         terms = jnp.dot(
-            jnp.concatenate([dense0, dense1], 0), jnp.concatenate([both, both], 0), preferred_element_type=F32
+            jnp.concatenate([dense(at0 >> shift), dense(at1 >> shift)], 0),
+            jnp.concatenate([both, both], 0),
+            preferred_element_type=F32,
         )
-        sum_even[row0] += terms[:block]
-        sum_odd[row1] += terms[block:]
-        return carry
-
-    for copy in copies:
-        copy.wait()
-    rows_in.wait()
-    lax.fori_loop(0, pairs, pair, 0, unroll=pairs)
+        sum_even[at0 & (out_ref.shape[0] - 1)] += terms[:block]
+        sum_odd[at1 & (out_ref.shape[0] - 1)] += terms[block:]
     for q in range(out_ref.shape[0]):
         total = sum_even[q] + pltpu.roll(sum_odd[q], fields, 1)
         out_ref[q] = total.T[:fields]
@@ -270,25 +252,19 @@
 
 def permute_kernel(owner_ref, x_ref, out_ref):
     ranks, pieces, block = x_ref.shape
-    rows = ranks * pieces
-    source = lax.broadcasted_iota(I32, (block, rows), 0)
-    spread = lax.broadcasted_iota(I32, (block, rows), 1) // pieces == source
-    owner = jnp.dot(
-        owner_ref[...].astype(BF16), spread.astype(F32).astype(BF16), preferred_element_type=F32
-    )[0:1]
-    half = lax.broadcasted_iota(I32, (1, rows), 1) % pieces
-    wanted = (owner.astype(I32) - 1) * pieces + half
-    chosen = lax.broadcasted_iota(I32, (rows, rows), 0) == jnp.broadcast_to(wanted, (rows, rows))
+    owner = owner_ref[0:1].astype(I32) - 1
+    chosen = lax.broadcasted_iota(I32, (ranks, ranks), 0) == jnp.broadcast_to(owner, (ranks, ranks))
     chosen = chosen.astype(F32).astype(BF16)
-    value = x_ref[...].reshape(rows, block)
+    value = jnp.concatenate([x_ref[:, k, :] for k in range(pieces)], 1)
     high = value.astype(BF16)
     left = value - high.astype(F32)
     middle = left.astype(BF16)
     low = (left - middle.astype(F32)).astype(BF16)
-    total = jnp.dot(chosen, high, preferred_element_type=F32)
-    total += jnp.dot(chosen, middle, preferred_element_type=F32)
-    total += jnp.dot(chosen, low, preferred_element_type=F32)
-    out_ref[...] = total.reshape(ranks, pieces, block)
+    total = jnp.dot(
+        jnp.concatenate([chosen] * 3, 1), jnp.concatenate([high, middle, low], 0), preferred_element_type=F32
+    )
+    for k in range(pieces):
+        out_ref[:, k, :] = total[:, k * block : (k + 1) * block]
 
 
 def hbm():
@@ -342,24 +318,26 @@
     )
     recv = exchange(send)
 
-    fluxes, slot = pl.pallas_call(
+    fluxes, place, onehot = pl.pallas_call(
         flux_kernel,
-        out_shape=(pltpu.VMEM((blocks // 2, block, 2 * fields), BF16), pltpu.HBM((blocks,), I32)),
+        out_shape=(
+            pltpu.VMEM((blocks // 2, block, 2 * fields), BF16),
+            pltpu.VMEM((8, blocks), I32),
+            pltpu.VMEM((2 * ranks, blocks), BF16),
+        ),
         in_specs=[hbm()] * 3 + [pl.BlockSpec(memory_space=pl.ANY)],
-        out_specs=(vmem(), hbm()),
+        out_specs=(vmem(), vmem(), vmem()),
         scratch_shapes=[
-            pltpu.SMEM((blocks,), I32),
-            pltpu.SMEM((blocks,), I32),
-            pltpu.SMEM((ranks,), I32),
+            pltpu.VMEM((1, blocks), I32),
             pltpu.VMEM((words, blocks), I32),
             pltpu.VMEM((blocks, fields, block), BF16),
             pltpu.VMEM((blocks, block), I32),
-            pltpu.SemaphoreType.DMA((4,)),
+            pltpu.SemaphoreType.DMA((3,)),
         ],
         compiler_params=params,
         cost_estimate=pl.CostEstimate(flops=10_000_000, bytes_accessed=4_000_000, transcendentals=0),
         name="flux",
-    )(in_hbm(coupler_owner), in_hbm(land_bits.T), in_hbm(atm_fields), send)
+    )(in_hbm(coupler_owner.reshape(1, blocks)), in_hbm(land_bits.T), in_hbm(atm_fields), send)
 
     sums, owner = pl.pallas_call(
         lambda *refs: remap_kernel(ranks, *refs),
@@ -367,19 +345,15 @@
             jax.ShapeDtypeStruct((ocean_blocks, fields, block), F32),
             jax.ShapeDtypeStruct((8, block), F32),
         ),
-        in_specs=[hbm(), vmem(), vmem()],
+        in_specs=[vmem()] * 4,
         out_specs=(vmem(), vmem()),
         scratch_shapes=[
-            pltpu.SMEM((blocks,), I32),
             pltpu.VMEM((ocean_blocks, block, 2 * fields), F32),
             pltpu.VMEM((ocean_blocks, block, 2 * fields), F32),
-            pltpu.VMEM((8, block), I32),
-            pltpu.SMEM((8, block), I32),
-            pltpu.SemaphoreType.DMA((2,)),
         ],
         compiler_params=params,
         name="remap",
-    )(in_hbm(slot), recv, fluxes)
+    )(place, onehot, recv, fluxes)
 
     pieces = ocean_blocks * fields // ranks
     spread = exchange(sums.reshape(ranks, pieces, block))

time: 61.8 us -> 61.5 us (level)
  no operation moved by 1% of the time
where the time goes in v4:
time: 61.5 us; the launch traced here: 61.3 us
  blocking collectives  28.4 us (46%)
  starting transfers between devices  11.5 us (19%)
  waiting for transfers between devices  11.2 us (18%)
  Pallas kernels  9.57 us (16%)
  local copies, waits for them, and re-layouts  0.66 us (1%)
    all_to_all x2, blocking collectives, exchange(): return lax.all_to_all(x, AXES, split_axis=0, concat_axis=0, tiled=True)  28.4 us
    all_to_all x1, starting transfers between devices, exchange(): return lax.all_to_all(x, AXES, split_axis=0, concat_axis=0, tiled=True)  11.5 us
    all_to_all x1, waiting for transfers between devices, exchange(): return lax.all_to_all(x, AXES, split_axis=0, concat_axis=0, tiled=True)  11.2 us
    pallas_call x1, Pallas kernels, on_device(): pl.pallas_call(flux_kernel, out_shape=(pltpu.VMEM((blocks // 2, block, 2...  3.37 us
    pallas_call x1, Pallas kernels, on_device(): pl.pallas_call(lambda *refs: remap_kernel(ranks, *refs), out_shape=(jax.S...  3.3 us
    pallas_call x1, Pallas kernels, on_device(): pl.pallas_call(lambda *refs: pack_kernel(ranks, ocean_blocks, *refs), out...  2.62 us
  transfers between devices with their start and end apart: 1, of which 1 were waited for; matrix products, arithmetic and copies ran while one was open for 0% of the time, Pallas kernels for 5%

profile of v4, /device:TPU:1, one launch (start us, length us, event | category | flops | bytes accessed | tf_op | source)
XLA Modules:
  0.0 61.3 jit_solution(6404060130728384205)
XLA Ops:
  0.0 2.6 %pack.1.sent_hbm = bf16[1152,2,128]{2,1,0:T(2,128)(2,1)} custom-call(s32[256]{0:T(256)} %refs_0_.1, s32[2,128]{1,0:T(2,128)} %bitcast.13, s32[2,128]{1,0:T(2,128)} %bitcast.14, bf16[1024,128]{1,0:T(8,128)(2,1)} %bitcast.11, s32[1024,128]{1,0:T(8,128)} %bitcast.9), custom_call_target="tpu_custom_call" | custom-call | tf_op jit(solution)/shard_map/pack/pallas_call | solution.py:295
  2.6 11.5 %all-to-all-start = ((bf16[1152,2,128]{2,1,0:T(2,128)(2,1)}), bf16[1152,2,128]{2,1,0:T(2,128)(2,1)S(1)}, u32[]{:S(2)}, u32[]{:S(2)}) async-start(bf16[1152,2,128]{2,1,0:T(2,128)(2,1)} %pack.1.sent_hbm), calls=%async_computation | async-start | bytes 1179648 | tf_op jit(solution)/shard_map/all_to_all | solution.py:283
  14.1 3.4 %flux.1 = (bf16[64,128,128]{2,1,0:T(8,128)(2,1)S(1)}, s32[8,128]{1,0:T(8,128)S(1)}, bf16[256,128]{1,0:T(8,128)(2,1)S(1)}) custom-call(s32[1,128]{1,0:T(1,128)} %bitcast.15, s32[5,128]{1,0:T(8,128)} %bitcast.12, bf16[128,64,128]{2,1,0:T(8,128)(2,1)} %atm_hbm.1, bf16[1152,2,128]{2,1,0:T(2,128)(2,1)} %pack.1.sent_hbm), custom_call_target="tpu_custom_call" | custom-call | flops 10000000 | bytes 4000000 | tf_op jit(solution)/shard_map/flux/pallas_call | solution.py:321
  17.5 11.2 %all-to-all-done.refs_2_ = bf16[1152,2,128]{2,1,0:T(2,128)(2,1)S(1)} async-done(((bf16[1152,2,128]{2,1,0:T(2,128)(2,1)}), bf16[1152,2,128]{2,1,0:T(2,128)(2,1)S(1)}, u32[]{:S(2)}, u32[]{:S(2)}) %all-to-all-start) | async-done | bytes 589856 | tf_op jit(solution)/shard_map/all_to_all | solution.py:283
  28.7 3.3 %remap.1 = (f32[4,64,128]{2,1,0:T(8,128)S(1)}, f32[8,128]{1,0:T(8,128)S(1)}) custom-call(s32[8,128]{1,0:T(8,128)S(1)} %get-tuple-element.10.refs_0_, bf16[256,128]{1,0:T(8,128)(2,1)S(1)} %get-tuple-element.11.refs_1_, bf16[1152,2,128]{2,1,0:T(2,128)(2,1)S(1)} %all-to-all-done.refs_2_, bf16[64,128,128]{2,1,0:T(8,128)(2,1)S(1)} %get-tuple-element.12.refs_3_), custom_call_target="tpu_custom_call" | custom-call | tf_op jit(solution)/shard_map/remap/pallas_call | solution.py:342
  32.0 14.2 %all_to_all.15.x_ref = f32[128,2,128]{2,1,0:T(2,128)S(1)} all-to-all(f32[128,2,128]{2,1,0:T(2,128)S(1)} %bitcast.8), channel_id=1, replica_groups=mesh['comp'=8,'cpl'=16] {'comp','cpl'}, dimensions={0} | all-to-all | bytes 262144 | tf_op jit(solution)/shard_map/all_to_all | solution.py:283
  46.2 0.3 permute.1
  46.5 14.2 %all_to_all.16 = f32[128,2,128]{2,1,0:T(2,128)S(1)} all-to-all(f32[128,2,128]{2,1,0:T(2,128)S(1)} %permute.1), channel_id=1, replica_groups=mesh['comp'=8,'cpl'=16] {'comp','cpl'}, dimensions={0} | all-to-all | bytes 262144 | tf_op jit(solution)/shard_map/all_to_all | solution.py:283
  60.6 0.7 %copy.9 = f32[4,64,128]{2,1,0:T(8,128)} copy(f32[4,64,128]{2,1,0:T(8,128)S(1)} %bitcast.10) | data formatting | bytes 262144
Async XLA Ops:
  2.6 26.0 %all-to-all-start = ((bf16[1152,2,128]{2,1,0:T(2,128)(2,1)}), bf16[1152,2,128]{2,1,0:T(2,128)(2,1)S(1)}, u32[]{:S(2)}, u32[]{:S(2)}) async-start(bf16[1152,2,128]{2,1,0:T(2,128)(2,1)} %pack.1.sent_hbm), calls=%async_computation | async-start | bytes 1179648 | tf_op jit(solution)/shard_map/all_to_all | solution.py:283

commit v5 on v4

--- a/solution.py
+++ b/solution.py
@@ -76,11 +76,13 @@
     row2_copy.wait()
     slot = (col2[...] & 1) * ranks + (col2[...] >> 1)
     entry = lax.broadcasted_iota(I32, (8, block), 0)
-    place = lax.broadcasted_iota(I32, (tiles, block), 0)
+    place = lax.broadcasted_iota(I32, (tiles, block), 0).astype(F32).astype(BF16)
+    slot = slot.astype(F32)
+    one, nothing = jnp.ones((), BF16), jnp.zeros((), BF16)
     onehot, values = [], []
     for h in range(halves):
-        same = jnp.broadcast_to(slot[h : h + 1], (tiles, block)) == place
-        onehot.append(jnp.where(same, 1.0, 0.0).astype(BF16))
+        same = jnp.broadcast_to(slot[h : h + 1].astype(BF16), (tiles, block)) == place
+        onehot.append(jnp.where(same, one, nothing))
         row = jnp.broadcast_to(row2[h : h + 1], (8, block))
         device = jnp.where(row >= 0, row // ocean_blocks + 1, 0)
         local = jnp.where(row >= 0, row % ocean_blocks, 0)
@@ -245,9 +247,13 @@
         )
         sum_even[at0 & (out_ref.shape[0] - 1)] += terms[:block]
         sum_odd[at1 & (out_ref.shape[0] - 1)] += terms[block:]
-    for q in range(out_ref.shape[0]):
-        total = sum_even[q] + pltpu.roll(sum_odd[q], fields, 1)
-        out_ref[q] = total.T[:fields]
+    low_lanes = lax.broadcasted_iota(I32, (block, 2 * fields), 1) < fields
+    for q in range(0, out_ref.shape[0], 2):
+        total = jnp.where(low_lanes, sum_even[q], sum_odd[q + 1])
+        total += pltpu.roll(jnp.where(low_lanes, sum_even[q + 1], sum_odd[q]), fields, 1)
+        both = total.T
+        out_ref[q] = both[:fields]
+        out_ref[q + 1] = both[fields:]
 
 
 def permute_kernel(owner_ref, x_ref, out_ref):

time: 61.5 us -> 61.5 us (level)
  transfers between devices with their start and end apart: 1 -> 1, of which waited for: 1 -> 1; matrix products, arithmetic and copies ran while one was open for 0% -> 0% of each run, Pallas kernels for 5% -> 6%
where the time goes in v5:
time: 61.5 us; the launch traced here: 61.2 us
  blocking collectives  28.4 us (46%)
  starting transfers between devices  11.5 us (19%)
  waiting for transfers between devices  11.2 us (18%)
  Pallas kernels  9.52 us (15%)
  local copies, waits for them, and re-layouts  0.66 us (1%)
    all_to_all x2, blocking collectives, exchange(): return lax.all_to_all(x, AXES, split_axis=0, concat_axis=0, tiled=True)  28.4 us
    all_to_all x1, starting transfers between devices, exchange(): return lax.all_to_all(x, AXES, split_axis=0, concat_axis=0, tiled=True)  11.5 us
    all_to_all x1, waiting for transfers between devices, exchange(): return lax.all_to_all(x, AXES, split_axis=0, concat_axis=0, tiled=True)  11.2 us
    pallas_call x1, Pallas kernels, on_device(): pl.pallas_call(flux_kernel, out_shape=(pltpu.VMEM((blocks // 2, block, 2...  3.37 us
    pallas_call x1, Pallas kernels, on_device(): pl.pallas_call(lambda *refs: remap_kernel(ranks, *refs), out_shape=(jax.S...  3.24 us
    pallas_call x1, Pallas kernels, on_device(): pl.pallas_call(lambda *refs: pack_kernel(ranks, ocean_blocks, *refs), out...  2.62 us
  transfers between devices with their start and end apart: 1, of which 1 were waited for; matrix products, arithmetic and copies ran while one was open for 0% of the time, Pallas kernels for 6%

profile of v5, /device:TPU:1, one launch (start us, length us, event | category | flops | bytes accessed | tf_op | source)
XLA Modules:
  0.0 61.2 jit_solution(9685619599857594866)
XLA Ops:
  0.0 2.6 %pack.1.sent_hbm = bf16[1152,2,128]{2,1,0:T(2,128)(2,1)} custom-call(s32[256]{0:T(256)} %refs_0_.1, s32[2,128]{1,0:T(2,128)} %bitcast.13, s32[2,128]{1,0:T(2,128)} %bitcast.14, bf16[1024,128]{1,0:T(8,128)(2,1)} %bitcast.11, s32[1024,128]{1,0:T(8,128)} %bitcast.9), custom_call_target="tpu_custom_call" | custom-call | tf_op jit(solution)/shard_map/pack/pallas_call | solution.py:301
  2.6 11.5 %all-to-all-start = ((bf16[1152,2,128]{2,1,0:T(2,128)(2,1)}), bf16[1152,2,128]{2,1,0:T(2,128)(2,1)S(1)}, u32[]{:S(2)}, u32[]{:S(2)}) async-start(bf16[1152,2,128]{2,1,0:T(2,128)(2,1)} %pack.1.sent_hbm), calls=%async_computation | async-start | bytes 1179648 | tf_op jit(solution)/shard_map/all_to_all | solution.py:289
  14.1 3.4 %flux.1 = (bf16[64,128,128]{2,1,0:T(8,128)(2,1)S(1)}, s32[8,128]{1,0:T(8,128)S(1)}, bf16[256,128]{1,0:T(8,128)(2,1)S(1)}) custom-call(s32[1,128]{1,0:T(1,128)} %bitcast.15, s32[5,128]{1,0:T(8,128)} %bitcast.12, bf16[128,64,128]{2,1,0:T(8,128)(2,1)} %atm_hbm.1, bf16[1152,2,128]{2,1,0:T(2,128)(2,1)} %pack.1.sent_hbm), custom_call_target="tpu_custom_call" | custom-call | flops 10000000 | bytes 4000000 | tf_op jit(solution)/shard_map/flux/pallas_call | solution.py:327
  17.5 11.2 %all-to-all-done.refs_2_ = bf16[1152,2,128]{2,1,0:T(2,128)(2,1)S(1)} async-done(((bf16[1152,2,128]{2,1,0:T(2,128)(2,1)}), bf16[1152,2,128]{2,1,0:T(2,128)(2,1)S(1)}, u32[]{:S(2)}, u32[]{:S(2)}) %all-to-all-start) | async-done | bytes 589856 | tf_op jit(solution)/shard_map/all_to_all | solution.py:289
  28.7 3.2 %remap.1 = (f32[4,64,128]{2,1,0:T(8,128)S(1)}, f32[8,128]{1,0:T(8,128)S(1)}) custom-call(s32[8,128]{1,0:T(8,128)S(1)} %get-tuple-element.10.refs_0_, bf16[256,128]{1,0:T(8,128)(2,1)S(1)} %get-tuple-element.11.refs_1_, bf16[1152,2,128]{2,1,0:T(2,128)(2,1)S(1)} %all-to-all-done.refs_2_, bf16[64,128,128]{2,1,0:T(8,128)(2,1)S(1)} %get-tuple-element.12.refs_3_), custom_call_target="tpu_custom_call" | custom-call | tf_op jit(solution)/shard_map/remap/pallas_call | solution.py:348
  31.9 14.2 %all_to_all.15.x_ref = f32[128,2,128]{2,1,0:T(2,128)S(1)} all-to-all(f32[128,2,128]{2,1,0:T(2,128)S(1)} %bitcast.8), channel_id=1, replica_groups=mesh['comp'=8,'cpl'=16] {'comp','cpl'}, dimensions={0} | all-to-all | bytes 262144 | tf_op jit(solution)/shard_map/all_to_all | solution.py:289
  46.1 0.3 permute.1
  46.4 14.2 %all_to_all.16 = f32[128,2,128]{2,1,0:T(2,128)S(1)} all-to-all(f32[128,2,128]{2,1,0:T(2,128)S(1)} %permute.1), channel_id=1, replica_groups=mesh['comp'=8,'cpl'=16] {'comp','cpl'}, dimensions={0} | all-to-all | bytes 262144 | tf_op jit(solution)/shard_map/all_to_all | solution.py:289
  60.6 0.7 %copy.9 = f32[4,64,128]{2,1,0:T(8,128)} copy(f32[4,64,128]{2,1,0:T(8,128)S(1)} %bitcast.10) | data formatting | bytes 262144
Async XLA Ops:
  2.6 26.0 %all-to-all-start = ((bf16[1152,2,128]{2,1,0:T(2,128)(2,1)}), bf16[1152,2,128]{2,1,0:T(2,128)(2,1)S(1)}, u32[]{:S(2)}, u32[]{:S(2)}) async-start(bf16[1152,2,128]{2,1,0:T(2,128)(2,1)} %pack.1.sent_hbm), calls=%async_computation | async-start | bytes 1179648 | tf_op jit(solution)/shard_map/all_to_all | solution.py:289

commit v6 on v3

--- a/solution.py
+++ b/solution.py
@@ -76,11 +76,13 @@
     row2_copy.wait()
     slot = (col2[...] & 1) * ranks + (col2[...] >> 1)
     entry = lax.broadcasted_iota(I32, (8, block), 0)
-    place = lax.broadcasted_iota(I32, (tiles, block), 0)
+    place = lax.broadcasted_iota(I32, (tiles, block), 0).astype(F32).astype(BF16)
+    slot = slot.astype(F32)
+    one, nothing = jnp.ones((), BF16), jnp.zeros((), BF16)
     onehot, values = [], []
     for h in range(halves):
-        same = jnp.broadcast_to(slot[h : h + 1], (tiles, block)) == place
-        onehot.append(jnp.where(same, 1.0, 0.0).astype(BF16))
+        same = jnp.broadcast_to(slot[h : h + 1].astype(BF16), (tiles, block)) == place
+        onehot.append(jnp.where(same, one, nothing))
         row = jnp.broadcast_to(row2[h : h + 1], (8, block))
         device = jnp.where(row >= 0, row // ocean_blocks + 1, 0)
         local = jnp.where(row >= 0, row % ocean_blocks, 0)
@@ -263,32 +265,30 @@
         copy.wait()
     rows_in.wait()
     lax.fori_loop(0, pairs, pair, 0, unroll=pairs)
-    for q in range(out_ref.shape[0]):
-        total = sum_even[q] + pltpu.roll(sum_odd[q], fields, 1)
-        out_ref[q] = total.T[:fields]
+    low_lanes = lax.broadcasted_iota(I32, (block, 2 * fields), 1) < fields
+    for q in range(0, out_ref.shape[0], 2):
+        total = jnp.where(low_lanes, sum_even[q], sum_odd[q + 1])
+        total += pltpu.roll(jnp.where(low_lanes, sum_even[q + 1], sum_odd[q]), fields, 1)
+        both = total.T
+        out_ref[q] = both[:fields]
+        out_ref[q + 1] = both[fields:]
 
 
 def permute_kernel(owner_ref, x_ref, out_ref):
     ranks, pieces, block = x_ref.shape
-    rows = ranks * pieces
-    source = lax.broadcasted_iota(I32, (block, rows), 0)
-    spread = lax.broadcasted_iota(I32, (block, rows), 1) // pieces == source
-    owner = jnp.dot(
-        owner_ref[...].astype(BF16), spread.astype(F32).astype(BF16), preferred_element_type=F32
-    )[0:1]
-    half = lax.broadcasted_iota(I32, (1, rows), 1) % pieces
-    wanted = (owner.astype(I32) - 1) * pieces + half
-    chosen = lax.broadcasted_iota(I32, (rows, rows), 0) == jnp.broadcast_to(wanted, (rows, rows))
+    owner = owner_ref[0:1].astype(I32) - 1
+    chosen = lax.broadcasted_iota(I32, (ranks, ranks), 0) == jnp.broadcast_to(owner, (ranks, ranks))
     chosen = chosen.astype(F32).astype(BF16)
-    value = x_ref[...].reshape(rows, block)
+    value = jnp.concatenate([x_ref[:, k, :] for k in range(pieces)], 1)
     high = value.astype(BF16)
     left = value - high.astype(F32)
     middle = left.astype(BF16)
     low = (left - middle.astype(F32)).astype(BF16)
-    total = jnp.dot(chosen, high, preferred_element_type=F32)
-    total += jnp.dot(chosen, middle, preferred_element_type=F32)
-    total += jnp.dot(chosen, low, preferred_element_type=F32)
-    out_ref[...] = total.reshape(ranks, pieces, block)
+    total = jnp.dot(
+        jnp.concatenate([chosen] * 3, 1), jnp.concatenate([high, middle, low], 0), preferred_element_type=F32
+    )
+    for k in range(pieces):
+        out_ref[:, k, :] = total[:, k * block : (k + 1) * block]
 
 
 def hbm():

time: 61.8 us -> 61.7 us (level)
  no operation moved by 1% of the time
where the time goes in v6:
time: 61.7 us; the launch traced here: 61.4 us
  blocking collectives  28.4 us (46%)
  starting transfers between devices  11.5 us (19%)
  waiting for transfers between devices  11.2 us (18%)
  Pallas kernels  9.73 us (16%)
  local copies, waits for them, and re-layouts  0.66 us (1%)
    all_to_all x2, blocking collectives, exchange(): return lax.all_to_all(x, AXES, split_axis=0, concat_axis=0, tiled=True)  28.4 us
    all_to_all x1, starting transfers between devices, exchange(): return lax.all_to_all(x, AXES, split_axis=0, concat_axis=0, tiled=True)  11.5 us
    all_to_all x1, waiting for transfers between devices, exchange(): return lax.all_to_all(x, AXES, split_axis=0, concat_axis=0, tiled=True)  11.2 us
    pallas_call x1, Pallas kernels, on_device(): pl.pallas_call(lambda *refs: remap_kernel(ranks, *refs), out_shape=(jax.S...  3.45 us
    pallas_call x1, Pallas kernels, on_device(): pl.pallas_call(flux_kernel, out_shape=(pltpu.VMEM((blocks // 2, block, 2...  3.37 us
    pallas_call x1, Pallas kernels, on_device(): pl.pallas_call(lambda *refs: pack_kernel(ranks, ocean_blocks, *refs), out...  2.62 us
  transfers between devices with their start and end apart: 1, of which 1 were waited for; matrix products, arithmetic and copies ran while one was open for 0% of the time, Pallas kernels for 5%

profile of v6, /device:TPU:1, one launch (start us, length us, event | category | flops | bytes accessed | tf_op | source)
XLA Modules:
  0.0 61.4 jit_solution(2100934366212523647)
XLA Ops:
  0.0 2.6 %pack.1.sent_hbm = bf16[1152,2,128]{2,1,0:T(2,128)(2,1)} custom-call(s32[256]{0:T(256)} %refs_0_.1, s32[2,128]{1,0:T(2,128)} %bitcast.12, s32[2,128]{1,0:T(2,128)} %bitcast.13, bf16[1024,128]{1,0:T(8,128)(2,1)} %bitcast.10, s32[1024,128]{1,0:T(8,128)} %bitcast.8), custom_call_target="tpu_custom_call" | custom-call | tf_op jit(solution)/shard_map/pack/pallas_call | solution.py:319
  2.6 11.5 %all-to-all-start = ((bf16[1152,2,128]{2,1,0:T(2,128)(2,1)}), bf16[1152,2,128]{2,1,0:T(2,128)(2,1)S(1)}, u32[]{:S(2)}, u32[]{:S(2)}) async-start(bf16[1152,2,128]{2,1,0:T(2,128)(2,1)} %pack.1.sent_hbm), calls=%async_computation | async-start | bytes 1179648 | tf_op jit(solution)/shard_map/all_to_all | solution.py:307
  14.1 3.4 %flux.1 = (bf16[64,128,128]{2,1,0:T(8,128)(2,1)S(1)}, s32[128]{0:T(128)}) custom-call(s32[128]{0:T(128)} %owner_hbm.1, s32[5,128]{1,0:T(8,128)} %bitcast.11, bf16[128,64,128]{2,1,0:T(8,128)(2,1)} %atm_hbm.1, bf16[1152,2,128]{2,1,0:T(2,128)(2,1)} %pack.1.sent_hbm), custom_call_target="tpu_custom_call" | custom-call | flops 10000000 | bytes 4000000 | tf_op jit(solution)/shard_map/flux/pallas_call | solution.py:345
  17.5 11.2 %all-to-all-done.refs_1_ = bf16[1152,2,128]{2,1,0:T(2,128)(2,1)S(1)} async-done(((bf16[1152,2,128]{2,1,0:T(2,128)(2,1)}), bf16[1152,2,128]{2,1,0:T(2,128)(2,1)S(1)}, u32[]{:S(2)}, u32[]{:S(2)}) %all-to-all-start) | async-done | bytes 589856 | tf_op jit(solution)/shard_map/all_to_all | solution.py:307
  28.7 3.4 %remap.1 = (f32[4,64,128]{2,1,0:T(8,128)S(1)}, f32[8,128]{1,0:T(8,128)S(1)}) custom-call(s32[128]{0:T(128)} %get-tuple-element.9.refs_0_, bf16[1152,2,128]{2,1,0:T(2,128)(2,1)S(1)} %all-to-all-done.refs_1_, bf16[64,128,128]{2,1,0:T(8,128)(2,1)S(1)} %get-tuple-element.10.refs_2_), custom_call_target="tpu_custom_call" | custom-call | tf_op jit(solution)/shard_map/remap/pallas_call | solution.py:364
  32.1 14.2 %all_to_all.15.x_ref = f32[128,2,128]{2,1,0:T(2,128)S(1)} all-to-all(f32[128,2,128]{2,1,0:T(2,128)S(1)} %bitcast.7), channel_id=1, replica_groups=mesh['comp'=8,'cpl'=16] {'comp','cpl'}, dimensions={0} | all-to-all | bytes 262144 | tf_op jit(solution)/shard_map/all_to_all | solution.py:307
  46.3 0.3 permute.1
  46.6 14.2 %all_to_all.16 = f32[128,2,128]{2,1,0:T(2,128)S(1)} all-to-all(f32[128,2,128]{2,1,0:T(2,128)S(1)} %permute.1), channel_id=1, replica_groups=mesh['comp'=8,'cpl'=16] {'comp','cpl'}, dimensions={0} | all-to-all | bytes 262144 | tf_op jit(solution)/shard_map/all_to_all | solution.py:307
  60.8 0.7 %copy.9 = f32[4,64,128]{2,1,0:T(8,128)} copy(f32[4,64,128]{2,1,0:T(8,128)S(1)} %bitcast.9) | data formatting | bytes 262144
Async XLA Ops:
  2.6 26.0 %all-to-all-start = ((bf16[1152,2,128]{2,1,0:T(2,128)(2,1)}), bf16[1152,2,128]{2,1,0:T(2,128)(2,1)S(1)}, u32[]{:S(2)}, u32[]{:S(2)}) async-start(bf16[1152,2,128]{2,1,0:T(2,128)(2,1)} %pack.1.sent_hbm), calls=%async_computation | async-start | bytes 1179648 | tf_op jit(solution)/shard_map/all_to_all | solution.py:307

commit v7 on v6

--- a/solution.py
+++ b/solution.py
@@ -214,19 +214,24 @@
     mine = lax.rem(me, other)
 
     def hear(c, carry):
-        local0, local1, device = carry
+        local0, local1 = carry
         info = recv[c * CHUNK + 2 * TILE_PAIRS].astype(F32)
         moved = pltpu.roll(info, lax.rem(c - mine + ranks, ranks), 1)
         local0 = jnp.maximum(local0, jnp.where(lane == c, moved, 0.0))
         local1 = jnp.maximum(local1, jnp.where(lane == (c ^ other), moved, 0.0))
-        return local0, local1, jnp.maximum(device, info)
+        return local0, local1
 
     zeros = jnp.zeros((2, block), F32)
-    local0, local1, device = lax.fori_loop(0, ranks, hear, (zeros, zeros, zeros), unroll=ranks)
+    local0, local1 = lax.fori_loop(0, ranks, hear, (zeros, zeros), unroll=ranks)
     padding = jnp.zeros((6, block), F32)
     rows_vmem[...] = jnp.concatenate([local0[1:2], local1[1:2], padding], 0).astype(I32)
     rows_in = pltpu.make_async_copy(rows_vmem, rows, sems.at[1])
     rows_in.start()
+
+    def hear_device(c, device):
+        return jnp.maximum(device, recv[c * CHUNK + 2 * TILE_PAIRS].astype(F32))
+
+    device = lax.fori_loop(0, ranks, hear_device, zeros, unroll=ranks)
     owner_ref[...] = jnp.concatenate([device, padding], 0)
     sum_even[...] = jnp.zeros_like(sum_even)
     sum_odd[...] = jnp.zeros_like(sum_odd)

time: 61.7 us -> 61.7 us (level)
  no operation moved by 1% of the time
where the time goes in v7:
time: 61.7 us; the launch traced here: 61.5 us
  blocking collectives  28.4 us (46%)
  starting transfers between devices  11.5 us (19%)
  waiting for transfers between devices  11.2 us (18%)
  Pallas kernels  9.73 us (16%)
  local copies, waits for them, and re-layouts  0.66 us (1%)
    all_to_all x2, blocking collectives, exchange(): return lax.all_to_all(x, AXES, split_axis=0, concat_axis=0, tiled=True)  28.4 us
    all_to_all x1, starting transfers between devices, exchange(): return lax.all_to_all(x, AXES, split_axis=0, concat_axis=0, tiled=True)  11.5 us
    all_to_all x1, waiting for transfers between devices, exchange(): return lax.all_to_all(x, AXES, split_axis=0, concat_axis=0, tiled=True)  11.2 us
    pallas_call x1, Pallas kernels, on_device(): pl.pallas_call(lambda *refs: remap_kernel(ranks, *refs), out_shape=(jax.S...  3.45 us
    pallas_call x1, Pallas kernels, on_device(): pl.pallas_call(flux_kernel, out_shape=(pltpu.VMEM((blocks // 2, block, 2...  3.37 us
    pallas_call x1, Pallas kernels, on_device(): pl.pallas_call(lambda *refs: pack_kernel(ranks, ocean_blocks, *refs), out...  2.62 us
  transfers between devices with their start and end apart: 1, of which 1 were waited for; matrix products, arithmetic and copies ran while one was open for 0% of the time, Pallas kernels for 5%

profile of v7, /device:TPU:1, one launch (start us, length us, event | category | flops | bytes accessed | tf_op | source)
XLA Modules:
  0.0 61.5 jit_solution(2389471829988079311)
XLA Ops:
  0.0 2.6 %pack.1.sent_hbm = bf16[1152,2,128]{2,1,0:T(2,128)(2,1)} custom-call(s32[256]{0:T(256)} %refs_0_.1, s32[2,128]{1,0:T(2,128)} %bitcast.12, s32[2,128]{1,0:T(2,128)} %bitcast.13, bf16[1024,128]{1,0:T(8,128)(2,1)} %bitcast.10, s32[1024,128]{1,0:T(8,128)} %bitcast.8), custom_call_target="tpu_custom_call" | custom-call | tf_op jit(solution)/shard_map/pack/pallas_call | solution.py:324
  2.6 11.5 %all-to-all-start = ((bf16[1152,2,128]{2,1,0:T(2,128)(2,1)}), bf16[1152,2,128]{2,1,0:T(2,128)(2,1)S(1)}, u32[]{:S(2)}, u32[]{:S(2)}) async-start(bf16[1152,2,128]{2,1,0:T(2,128)(2,1)} %pack.1.sent_hbm), calls=%async_computation | async-start | bytes 1179648 | tf_op jit(solution)/shard_map/all_to_all | solution.py:312
  14.1 3.4 %flux.1 = (bf16[64,128,128]{2,1,0:T(8,128)(2,1)S(1)}, s32[128]{0:T(128)}) custom-call(s32[128]{0:T(128)} %owner_hbm.1, s32[5,128]{1,0:T(8,128)} %bitcast.11, bf16[128,64,128]{2,1,0:T(8,128)(2,1)} %atm_hbm.1, bf16[1152,2,128]{2,1,0:T(2,128)(2,1)} %pack.1.sent_hbm), custom_call_target="tpu_custom_call" | custom-call | flops 10000000 | bytes 4000000 | tf_op jit(solution)/shard_map/flux/pallas_call | solution.py:350
  17.5 11.2 %all-to-all-done.refs_1_ = bf16[1152,2,128]{2,1,0:T(2,128)(2,1)S(1)} async-done(((bf16[1152,2,128]{2,1,0:T(2,128)(2,1)}), bf16[1152,2,128]{2,1,0:T(2,128)(2,1)S(1)}, u32[]{:S(2)}, u32[]{:S(2)}) %all-to-all-start) | async-done | bytes 589856 | tf_op jit(solution)/shard_map/all_to_all | solution.py:312
  28.7 3.5 %remap.1 = (f32[4,64,128]{2,1,0:T(8,128)S(1)}, f32[8,128]{1,0:T(8,128)S(1)}) custom-call(s32[128]{0:T(128)} %get-tuple-element.9.refs_0_, bf16[1152,2,128]{2,1,0:T(2,128)(2,1)S(1)} %all-to-all-done.refs_1_, bf16[64,128,128]{2,1,0:T(8,128)(2,1)S(1)} %get-tuple-element.10.refs_2_), custom_call_target="tpu_custom_call" | custom-call | tf_op jit(solution)/shard_map/remap/pallas_call | solution.py:369
  32.1 14.2 %all_to_all.15.x_ref = f32[128,2,128]{2,1,0:T(2,128)S(1)} all-to-all(f32[128,2,128]{2,1,0:T(2,128)S(1)} %bitcast.7), channel_id=1, replica_groups=mesh['comp'=8,'cpl'=16] {'comp','cpl'}, dimensions={0} | all-to-all | bytes 262144 | tf_op jit(solution)/shard_map/all_to_all | solution.py:312
  46.3 0.3 permute.1
  46.6 14.2 %all_to_all.16 = f32[128,2,128]{2,1,0:T(2,128)S(1)} all-to-all(f32[128,2,128]{2,1,0:T(2,128)S(1)} %permute.1), channel_id=1, replica_groups=mesh['comp'=8,'cpl'=16] {'comp','cpl'}, dimensions={0} | all-to-all | bytes 262144 | tf_op jit(solution)/shard_map/all_to_all | solution.py:312
  60.8 0.7 %copy.9 = f32[4,64,128]{2,1,0:T(8,128)} copy(f32[4,64,128]{2,1,0:T(8,128)S(1)} %bitcast.9) | data formatting | bytes 262144
Async XLA Ops:
  2.6 26.0 %all-to-all-start = ((bf16[1152,2,128]{2,1,0:T(2,128)(2,1)}), bf16[1152,2,128]{2,1,0:T(2,128)(2,1)S(1)}, u32[]{:S(2)}, u32[]{:S(2)}) async-start(bf16[1152,2,128]{2,1,0:T(2,128)(2,1)} %pack.1.sent_hbm), calls=%async_computation | async-start | bytes 1179648 | tf_op jit(solution)/shard_map/all_to_all | solution.py:312
